TPU v7x, 512 devices: a whole 4x4x16 slice. The times are simulated.
512 devices in a mesh: gx: 128 (over z, y_lo, x), gy: 4 (over y_hi, core).
Axes of the slice: x: 4, y: 4 (y_hi: 2, y_lo: 2; y = y_hi * 2 + y_lo), z: 16, core: 2. Of those that a mesh axis runs over, the one named last changes fastest.
Arguments:
- fine_cotangent: float32 [2, 2048, 1024], P(None, 'gx', 'gy'), may hold values from -6 to 6
- coarse_cotangent: float32 [2, 2048, 1024], P(None, 'gx', 'gy'), may hold values from -6 to 6
- upstream_x: int32 [3, 8], replicated, may hold values from -256 to 256, as said below
- upstream_y: int32 [3, 16], replicated, may hold values from -32 to 32, as said below
- fractions: float32 [3, 2], replicated, may hold values from 0.05 to 0.95
Outputs:
- difference: float32 [2, 2048, 1024], P(None, 'gx', 'gy')
Inputs may be any that keep to these rules, and one draw needn't show every extreme that they name: `upstream_x`: each entry lies in -256 to 256; both ends occur in every draw. `upstream_y`: each entry lies in -32 to 32; both ends occur in every draw.
All inputs are finite; a program needn't handle non-finite values.
Results may differ from a plain program's by a relative error of at most 0.00002.
Values sent between devices are 32-bit elements; how exact they have to be, the bound alone decides.
A program may use at most 64 MiB of HBM per device.

v0:
```python
import jax
import jax.numpy as jnp
from jax import lax
from jax.sharding import PartitionSpec as P

LINE = 128
MAXDY = 32


def shifted(block, axis, distance):
    devices = range(lax.axis_size(axis))
    route = [((i - distance) % len(devices), i) for i in devices]
    return lax.ppermute(block, axis, route)


def padded(cells, sides, width):
    for axis, dim in sides:
        count = lax.axis_size(axis)
        head = lax.slice_in_dim(cells, 0, width, axis=dim)
        tail = lax.slice_in_dim(cells, cells.shape[dim] - width, cells.shape[dim], axis=dim)
        cells = jnp.concatenate(
            [
                lax.ppermute(tail, axis, [(i, (i + 1) % count) for i in range(count)]),
                cells,
                lax.ppermute(head, axis, [((i + 1) % count, i) for i in range(count)]),
            ],
            axis=dim,
        )
    return cells


def cubic_weights(fraction):
    position = 1.0 - fraction
    return (
        -position * (position - 1.0) * (position - 2.0) / 6.0,
        (position + 1.0) * (position - 1.0) * (position - 2.0) / 2.0,
        -(position + 1.0) * position * (position - 2.0) / 2.0,
        (position + 1.0) * position * (position - 1.0) / 6.0,
    )


def apply_taps(window, weights, along_axis, length):
    summed = weights[0] * lax.slice_in_dim(window, 3, 3 + length, axis=along_axis)
    for tap_index in range(1, 4):
        summed = summed + weights[tap_index] * lax.slice_in_dim(
            window, 3 - tap_index, 3 - tap_index + length, axis=along_axis
        )
    return summed


def fetch_slab(incoming, offset):
    return shifted(incoming, "gx", offset)


def sweep_x(incoming, shifts, weights):
    level_count, slab_width, row_length = incoming.shape
    blocks = row_length // LINE
    span_devices = min(16, lax.axis_size("gx") // 8)
    local_shifts = lax.dynamic_slice_in_dim(shifts, lax.axis_index("gy") * blocks, blocks)
    rim_cells = (span_devices + 1) * slab_width
    lower_side = [fetch_slab(incoming, distance) for distance in range(span_devices + 1, 0, -1)]
    upper_side = [fetch_slab(incoming, -distance) for distance in range(1, span_devices + 2)]
    extended = jnp.concatenate(lower_side + [incoming] + upper_side, axis=1)
    pieces = []
    for block_index in range(blocks):
        column = lax.slice_in_dim(extended, block_index * LINE, (block_index + 1) * LINE, axis=2)
        window = lax.dynamic_slice_in_dim(
            column, rim_cells + local_shifts[block_index] - 1, slab_width + 3, 1
        )
        pieces.append(apply_taps(window, weights, 1, slab_width))
    return jnp.concatenate(pieces, axis=2)


def sweep_y(incoming, shifts, weights):
    level_count, slab_width, row_length = incoming.shape
    rim_cells = MAXDY + 2
    strip_index = lax.axis_index("gx") * slab_width // LINE
    offset = lax.dynamic_index_in_dim(shifts, strip_index, 0, keepdims=False)
    extended = padded(incoming, (("gy", 2),), rim_cells)
    window = lax.dynamic_slice_in_dim(extended, rim_cells + offset - 1, row_length + 3, 2)
    return apply_taps(window, weights, 2, row_length)


def local(fine_cotangent, coarse_cotangent, upstream_x, upstream_y, fractions):

    def adjoint_pass(incoming, pass_row):
        along_x = cubic_weights(fractions[pass_row, 0])
        along_y = cubic_weights(fractions[pass_row, 1])
        swept = sweep_x(incoming, upstream_x[pass_row], along_x)
        return sweep_y(swept, upstream_y[pass_row], along_y)

    fine_field = adjoint_pass(adjoint_pass(fine_cotangent, 1), 0)
    coarse_field = adjoint_pass(coarse_cotangent, 2)
    return fine_field - coarse_field


def solution(mesh):
    placed = (P(None, "gx", "gy"), P(None, "gx", "gy"), P(), P(), P())
    return jax.shard_map(
        local, mesh=mesh, in_specs=placed, out_specs=P(None, "gx", "gy"), check_vma=False
    )
```

profile of v0, /device:TPU:1, one launch (start us, length us, event | category | flops | bytes accessed | tf_op | source)
XLA Modules:
  0.0 527.8 jit_solution(15883572054847992783)
XLA Ops:
  0.0 6.8 %collective-permute-start = (f32[2,16,256]{2,1,0:T(8,128)}, f32[2,16,256]{2,1,0:T(8,128)S(1)}, u32[]{:S(2)}, u32[]{:S(2)}) collective-permute-start(f32[2,16,256]{2,1,0:T(8,128)} %param.5), channel_id=1, source_target_pairs={{444,0},{448,4},{452,8},{456,12},{460,16},{464,20},{468,24},{472,2... | collective-permute-start | bytes 98312 | tf_op jit(solution)/shard_map/ppermute | solution.py:13
  6.8 6.1 %collective-permute-start.1 = (f32[2,16,256]{2,1,0:T(8,128)}, f32[2,16,256]{2,1,0:T(8,128)S(1)}, u32[]{:S(2)}, u32[]{:S(2)}) collective-permute-start(f32[2,16,256]{2,1,0:T(8,128)} %param.5), channel_id=1, source_target_pairs={{448,0},{452,4},{456,8},{460,12},{464,16},{468,20},{472,24},{476,2... | collective-permute-start | bytes 98312 | tf_op jit(solution)/shard_map/ppermute | solution.py:13
  12.9 7.0 %collective-permute-start.2 = (f32[2,16,256]{2,1,0:T(8,128)}, f32[2,16,256]{2,1,0:T(8,128)S(1)}, u32[]{:S(2)}, u32[]{:S(2)}) collective-permute-start(f32[2,16,256]{2,1,0:T(8,128)} %param.5), channel_id=1, source_target_pairs={{452,0},{456,4},{460,8},{464,12},{468,16},{472,20},{476,24},{480,2... | collective-permute-start | bytes 98312 | tf_op jit(solution)/shard_map/ppermute | solution.py:13
  24.8 5.1 collective-permute-start.4
  81.4 5.7 %collective-permute-start.10 = (f32[2,16,256]{2,1,0:T(8,128)}, f32[2,16,256]{2,1,0:T(8,128)S(1)}, u32[]{:S(2)}, u32[]{:S(2)}) collective-permute-start(f32[2,16,256]{2,1,0:T(8,128)} %param.5), channel_id=1, source_target_pairs={{484,0},{488,4},{492,8},{496,12},{500,16},{504,20},{508,24},{0,28}... | collective-permute-start | bytes 98312 | tf_op jit(solution)/shard_map/ppermute | solution.py:13
  104.2 7.6 %collective-permute-start.17 = (f32[2,16,256]{2,1,0:T(8,128)S(1)}, f32[2,16,256]{2,1,0:T(8,128)S(1)}, u32[]{:S(2)}, u32[]{:S(2)}) collective-permute-start(f32[2,16,256]{2,1,0:T(8,128)S(1)} %copy-done), channel_id=1, source_target_pairs={{4,0},{8,4},{12,8},{16,12},{20,16},{24,20},{28,24},{32,28},{36,32}... | collective-permute-start | bytes 98312 | tf_op jit(solution)/shard_map/ppermute | solution.py:13
  124.6 5.5 %collective-permute-start.22 = (f32[2,16,256]{2,1,0:T(8,128)S(1)}, f32[2,16,256]{2,1,0:T(8,128)S(1)}, u32[]{:S(2)}, u32[]{:S(2)}) collective-permute-start(f32[2,16,256]{2,1,0:T(8,128)S(1)} %copy-done), channel_id=1, source_target_pairs={{24,0},{28,4},{32,8},{36,12},{40,16},{44,20},{48,24},{52,28},{56,3... | collective-permute-start | bytes 98312 | tf_op jit(solution)/shard_map/ppermute | solution.py:13
  135.9 7.1 %collective-permute-start.25 = (f32[2,16,256]{2,1,0:T(8,128)S(1)}, f32[2,16,256]{2,1,0:T(8,128)S(1)}, u32[]{:S(2)}, u32[]{:S(2)}) collective-permute-start(f32[2,16,256]{2,1,0:T(8,128)S(1)} %copy-done), channel_id=1, source_target_pairs={{36,0},{40,4},{44,8},{48,12},{52,16},{56,20},{60,24},{64,28},{68,3... | collective-permute-start | bytes 98312 | tf_op jit(solution)/shard_map/ppermute | solution.py:13
  165.7 9.5 %collective-permute-start.33 = (f32[2,16,256]{2,1,0:T(8,128)S(1)}, f32[2,16,256]{2,1,0:T(8,128)S(1)}, u32[]{:S(2)}, u32[]{:S(2)}) collective-permute-start(f32[2,16,256]{2,1,0:T(8,128)S(1)} %copy-done), channel_id=1, source_target_pairs={{68,0},{72,4},{76,8},{80,12},{84,16},{88,20},{92,24},{96,28},{100,... | collective-permute-start | bytes 98312 | tf_op jit(solution)/shard_map/ppermute | solution.py:13
  179.5 8.7 %collective-permute-start.74 = (f32[2,16,256]{2,1,0:T(8,128)S(1)}, f32[2,16,256]{2,1,0:T(8,128)S(1)}, u32[]{:S(2)}, u32[]{:S(2)}) collective-permute-start(f32[2,16,256]{2,1,0:T(8,128)S(1)} %copy-done.1), channel_id=1, source_target_pairs={{452,0},{456,4},{460,8},{464,12},{468,16},{472,20},{476,24},{480,2... | collective-permute-start | bytes 98312 | tf_op jit(solution)/shard_map/ppermute | solution.py:13
  193.8 5.8 %collective-permute-start.77 = (f32[2,16,256]{2,1,0:T(8,128)S(1)}, f32[2,16,256]{2,1,0:T(8,128)S(1)}, u32[]{:S(2)}, u32[]{:S(2)}) collective-permute-start(f32[2,16,256]{2,1,0:T(8,128)S(1)} %copy-done.1), channel_id=1, source_target_pairs={{464,0},{468,4},{472,8},{476,12},{480,16},{484,20},{488,24},{492,2... | collective-permute-start | bytes 98312 | tf_op jit(solution)/shard_map/ppermute | solution.py:13
  203.4 5.9 %collective-permute-start.79 = (f32[2,16,256]{2,1,0:T(8,128)S(1)}, f32[2,16,256]{2,1,0:T(8,128)S(1)}, u32[]{:S(2)}, u32[]{:S(2)}) collective-permute-start(f32[2,16,256]{2,1,0:T(8,128)S(1)} %copy-done.1), channel_id=1, source_target_pairs={{472,0},{476,4},{480,8},{484,12},{488,16},{492,20},{496,24},{500,2... | collective-permute-start | bytes 98312 | tf_op jit(solution)/shard_map/ppermute | solution.py:13
  213.9 5.7 %collective-permute-start.82 = (f32[2,16,256]{2,1,0:T(8,128)S(1)}, f32[2,16,256]{2,1,0:T(8,128)S(1)}, u32[]{:S(2)}, u32[]{:S(2)}) collective-permute-start(f32[2,16,256]{2,1,0:T(8,128)S(1)} %copy-done.1), channel_id=1, source_target_pairs={{484,0},{488,4},{492,8},{496,12},{500,16},{504,20},{508,24},{0,28}... | collective-permute-start | bytes 98312 | tf_op jit(solution)/shard_map/ppermute | solution.py:13
  237.6 7.6 %collective-permute-start.89 = (f32[2,16,256]{2,1,0:T(8,128)S(1)}, f32[2,16,256]{2,1,0:T(8,128)S(1)}, u32[]{:S(2)}, u32[]{:S(2)}) collective-permute-start(f32[2,16,256]{2,1,0:T(8,128)S(1)} %copy-done.1), channel_id=1, source_target_pairs={{4,0},{8,4},{12,8},{16,12},{20,16},{24,20},{28,24},{32,28},{36,32}... | collective-permute-start | bytes 98312 | tf_op jit(solution)/shard_map/ppermute | solution.py:13
  257.1 5.5 %collective-permute-start.94 = (f32[2,16,256]{2,1,0:T(8,128)S(1)}, f32[2,16,256]{2,1,0:T(8,128)S(1)}, u32[]{:S(2)}, u32[]{:S(2)}) collective-permute-start(f32[2,16,256]{2,1,0:T(8,128)S(1)} %copy-done.1), channel_id=1, source_target_pairs={{24,0},{28,4},{32,8},{36,12},{40,16},{44,20},{48,24},{52,28},{56,3... | collective-permute-start | bytes 98312 | tf_op jit(solution)/shard_map/ppermute | solution.py:13
  269.3 6.2 %collective-permute-start.97 = (f32[2,16,256]{2,1,0:T(8,128)S(1)}, f32[2,16,256]{2,1,0:T(8,128)S(1)}, u32[]{:S(2)}, u32[]{:S(2)}) collective-permute-start(f32[2,16,256]{2,1,0:T(8,128)S(1)} %copy-done.1), channel_id=1, source_target_pairs={{36,0},{40,4},{44,8},{48,12},{52,16},{56,20},{60,24},{64,28},{68,3... | collective-permute-start | bytes 98312 | tf_op jit(solution)/shard_map/ppermute | solution.py:13
  277.5 5.0 collective-permute-start.99
  285.8 5.1 collective-permute-start.101
  299.6 9.0 %collective-permute-start.105 = (f32[2,16,256]{2,1,0:T(8,128)S(1)}, f32[2,16,256]{2,1,0:T(8,128)S(1)}, u32[]{:S(2)}, u32[]{:S(2)}) collective-permute-start(f32[2,16,256]{2,1,0:T(8,128)S(1)} %copy-done.1), channel_id=1, source_target_pairs={{68,0},{72,4},{76,8},{80,12},{84,16},{88,20},{92,24},{96,28},{100,... | collective-permute-start | bytes 98312 | tf_op jit(solution)/shard_map/ppermute | solution.py:13
  308.7 24.0 %collective-permute-start.34 = (f32[2,16,34]{2,1,0:T(8,128)S(1)}, f32[2,16,34]{2,1,0:T(8,128)S(1)}, u32[]{:S(2)}, u32[]{:S(2)}) collective-permute-start(f32[2,16,34]{2,1,0:T(8,128)S(1)} %slice.271), channel_id=1, source_target_pairs={{0,1},{1,2},{2,3},{3,0},{4,5},{5,6},{6,7},{7,4},{8,9},{9,10},{10,1... | collective-permute-start | bytes 13064 | tf_op jit(solution)/shard_map/ppermute | solution.py:23
  335.0 11.9 %collective-permute-start.106 = (f32[2,16,34]{2,1,0:T(8,128)S(1)}, f32[2,16,34]{2,1,0:T(8,128)S(1)}, u32[]{:S(2)}, u32[]{:S(2)}) collective-permute-start(f32[2,16,34]{2,1,0:T(8,128)S(1)} %slice.287), channel_id=1, source_target_pairs={{0,1},{1,2},{2,3},{3,0},{4,5},{5,6},{6,7},{7,4},{8,9},{9,10},{10,1... | collective-permute-start | bytes 13064 | tf_op jit(solution)/shard_map/ppermute | solution.py:23
  347.2 5.5 %collective-permute-start.36 = (f32[2,16,256]{2,1,0:T(8,128)S(1)}, f32[2,16,256]{2,1,0:T(8,128)S(1)}, u32[]{:S(2)}, u32[]{:S(2)}) collective-permute-start(f32[2,16,256]{2,1,0:T(8,128)S(1)} %fusion.7), channel_id=1, source_target_pairs={{444,0},{448,4},{452,8},{456,12},{460,16},{464,20},{468,24},{472,2... | collective-permute-start | bytes 98312 | tf_op jit(solution)/shard_map/ppermute | solution.py:13
  352.7 17.1 %collective-permute-start.107 = (f32[2,16,34]{2,1,0:T(8,128)S(1)}, f32[2,16,34]{2,1,0:T(8,128)S(1)}, u32[]{:S(2)}, u32[]{:S(2)}) collective-permute-start(f32[2,16,34]{2,1,0:T(8,128)S(1)} %bitcast.45), channel_id=1, source_target_pairs={{1,0},{2,1},{3,2},{0,3},{5,4},{6,5},{7,6},{4,7},{9,8},{10,9},{11,1... | collective-permute-start | bytes 13064 | tf_op jit(solution)/shard_map/ppermute | solution.py:25
  374.5 6.5 %collective-permute-start.38 = (f32[2,16,256]{2,1,0:T(8,128)S(1)}, f32[2,16,256]{2,1,0:T(8,128)S(1)}, u32[]{:S(2)}, u32[]{:S(2)}) collective-permute-start(f32[2,16,256]{2,1,0:T(8,128)S(1)} %fusion.7), channel_id=1, source_target_pairs={{452,0},{456,4},{460,8},{464,12},{468,16},{472,20},{476,24},{480,2... | collective-permute-start | bytes 98312 | tf_op jit(solution)/shard_map/ppermute | solution.py:13
  381.0 6.0 %collective-permute-start.39 = (f32[2,16,256]{2,1,0:T(8,128)S(1)}, f32[2,16,256]{2,1,0:T(8,128)S(1)}, u32[]{:S(2)}, u32[]{:S(2)}) collective-permute-start(f32[2,16,256]{2,1,0:T(8,128)S(1)} %fusion.7), channel_id=1, source_target_pairs={{456,0},{460,4},{464,8},{468,12},{472,16},{476,20},{480,24},{484,2... | collective-permute-start | bytes 98312 | tf_op jit(solution)/shard_map/ppermute | solution.py:13
  391.8 5.5 %collective-permute-start.41 = (f32[2,16,256]{2,1,0:T(8,128)S(1)}, f32[2,16,256]{2,1,0:T(8,128)S(1)}, u32[]{:S(2)}, u32[]{:S(2)}) collective-permute-start(f32[2,16,256]{2,1,0:T(8,128)S(1)} %fusion.7), channel_id=1, source_target_pairs={{464,0},{468,4},{472,8},{476,12},{480,16},{484,20},{488,24},{492,2... | collective-permute-start | bytes 98312 | tf_op jit(solution)/shard_map/ppermute | solution.py:13
  434.0 7.6 %collective-permute-start.53 = (f32[2,16,256]{2,1,0:T(8,128)S(1)}, f32[2,16,256]{2,1,0:T(8,128)S(1)}, u32[]{:S(2)}, u32[]{:S(2)}) collective-permute-start(f32[2,16,256]{2,1,0:T(8,128)S(1)} %fusion.7), channel_id=1, source_target_pairs={{4,0},{8,4},{12,8},{16,12},{20,16},{24,20},{28,24},{32,28},{36,32}... | collective-permute-start | bytes 98312 | tf_op jit(solution)/shard_map/ppermute | solution.py:13
  453.6 5.2 collective-permute-start.58
  464.9 6.6 %collective-permute-start.61 = (f32[2,16,256]{2,1,0:T(8,128)S(1)}, f32[2,16,256]{2,1,0:T(8,128)S(1)}, u32[]{:S(2)}, u32[]{:S(2)}) collective-permute-start(f32[2,16,256]{2,1,0:T(8,128)S(1)} %fusion.7), channel_id=1, source_target_pairs={{36,0},{40,4},{44,8},{48,12},{52,16},{56,20},{60,24},{64,28},{68,3... | collective-permute-start | bytes 98312 | tf_op jit(solution)/shard_map/ppermute | solution.py:13
  473.5 5.3 %collective-permute-start.63 = (f32[2,16,256]{2,1,0:T(8,128)S(1)}, f32[2,16,256]{2,1,0:T(8,128)S(1)}, u32[]{:S(2)}, u32[]{:S(2)}) collective-permute-start(f32[2,16,256]{2,1,0:T(8,128)S(1)} %fusion.7), channel_id=1, source_target_pairs={{44,0},{48,4},{52,8},{56,12},{60,16},{64,20},{68,24},{72,28},{76,3... | collective-permute-start | bytes 98312 | tf_op jit(solution)/shard_map/ppermute | solution.py:13
  494.6 10.0 %collective-permute-start.69 = (f32[2,16,256]{2,1,0:T(8,128)S(1)}, f32[2,16,256]{2,1,0:T(8,128)S(1)}, u32[]{:S(2)}, u32[]{:S(2)}) collective-permute-start(f32[2,16,256]{2,1,0:T(8,128)S(1)} %fusion.7), channel_id=1, source_target_pairs={{68,0},{72,4},{76,8},{80,12},{84,16},{88,20},{92,24},{96,28},{100,... | collective-permute-start | bytes 98312 | tf_op jit(solution)/shard_map/ppermute | solution.py:13
  505.8 14.5 %collective-permute-start.70 = (f32[2,16,34]{2,1,0:T(8,128)S(1)}, f32[2,16,34]{2,1,0:T(8,128)S(1)}, u32[]{:S(2)}, u32[]{:S(2)}) collective-permute-start(f32[2,16,34]{2,1,0:T(8,128)S(1)} %slice.279), channel_id=1, source_target_pairs={{0,1},{1,2},{2,3},{3,0},{4,5},{5,6},{6,7},{7,4},{8,9},{9,10},{10,1... | collective-permute-start | bytes 13064 | tf_op jit(solution)/shard_map/ppermute | solution.py:23
  (320 shorter events, 246.7 us)
Async XLA Ops:
  0.0 64.4 %collective-permute-start = (f32[2,16,256]{2,1,0:T(8,128)}, f32[2,16,256]{2,1,0:T(8,128)S(1)}, u32[]{:S(2)}, u32[]{:S(2)}) collective-permute-start(f32[2,16,256]{2,1,0:T(8,128)} %param.5), channel_id=1, source_target_pairs={{444,0},{448,4},{452,8},{456,12},{460,16},{464,20},{468,24},{472,2... | collective-permute-start | bytes 98312 | tf_op jit(solution)/shard_map/ppermute | solution.py:13
  6.8 61.3 %collective-permute-start.1 = (f32[2,16,256]{2,1,0:T(8,128)}, f32[2,16,256]{2,1,0:T(8,128)S(1)}, u32[]{:S(2)}, u32[]{:S(2)}) collective-permute-start(f32[2,16,256]{2,1,0:T(8,128)} %param.5), channel_id=1, source_target_pairs={{448,0},{452,4},{456,8},{460,12},{464,16},{468,20},{472,24},{476,2... | collective-permute-start | bytes 98312 | tf_op jit(solution)/shard_map/ppermute | solution.py:13
  12.9 59.4 %collective-permute-start.2 = (f32[2,16,256]{2,1,0:T(8,128)}, f32[2,16,256]{2,1,0:T(8,128)S(1)}, u32[]{:S(2)}, u32[]{:S(2)}) collective-permute-start(f32[2,16,256]{2,1,0:T(8,128)} %param.5), channel_id=1, source_target_pairs={{452,0},{456,4},{460,8},{464,12},{468,16},{472,20},{476,24},{480,2... | collective-permute-start | bytes 98312 | tf_op jit(solution)/shard_map/ppermute | solution.py:13
  19.9 56.9 %collective-permute-start.3 = (f32[2,16,256]{2,1,0:T(8,128)}, f32[2,16,256]{2,1,0:T(8,128)S(1)}, u32[]{:S(2)}, u32[]{:S(2)}) collective-permute-start(f32[2,16,256]{2,1,0:T(8,128)} %param.5), channel_id=1, source_target_pairs={{456,0},{460,4},{464,8},{468,12},{472,16},{476,20},{480,24},{484,2... | collective-permute-start | bytes 98312 | tf_op jit(solution)/shard_map/ppermute | solution.py:13
  24.8 53.9 %collective-permute-start.4 = (f32[2,16,256]{2,1,0:T(8,128)}, f32[2,16,256]{2,1,0:T(8,128)S(1)}, u32[]{:S(2)}, u32[]{:S(2)}) collective-permute-start(f32[2,16,256]{2,1,0:T(8,128)} %param.5), channel_id=1, source_target_pairs={{460,0},{464,4},{468,8},{472,12},{476,16},{480,20},{484,24},{488,2... | collective-permute-start | bytes 98312 | tf_op jit(solution)/shard_map/ppermute | solution.py:13
  91.7 20.2 %collective-permute-start.13 = (f32[2,16,256]{2,1,0:T(8,128)}, f32[2,16,256]{2,1,0:T(8,128)S(1)}, u32[]{:S(2)}, u32[]{:S(2)}) collective-permute-start(f32[2,16,256]{2,1,0:T(8,128)} %param.5), channel_id=1, source_target_pairs={{496,0},{500,4},{504,8},{508,12},{0,16},{4,20},{8,24},{12,28},{16,... | collective-permute-start | bytes 98312 | tf_op jit(solution)/shard_map/ppermute | solution.py:13
  104.2 20.3 %collective-permute-start.17 = (f32[2,16,256]{2,1,0:T(8,128)S(1)}, f32[2,16,256]{2,1,0:T(8,128)S(1)}, u32[]{:S(2)}, u32[]{:S(2)}) collective-permute-start(f32[2,16,256]{2,1,0:T(8,128)S(1)} %copy-done), channel_id=1, source_target_pairs={{4,0},{8,4},{12,8},{16,12},{20,16},{24,20},{28,24},{32,28},{36,32}... | collective-permute-start | bytes 98312 | tf_op jit(solution)/shard_map/ppermute | solution.py:13
  120.6 22.4 %collective-permute-start.21 = (f32[2,16,256]{2,1,0:T(8,128)S(1)}, f32[2,16,256]{2,1,0:T(8,128)S(1)}, u32[]{:S(2)}, u32[]{:S(2)}) collective-permute-start(f32[2,16,256]{2,1,0:T(8,128)S(1)} %copy-done), channel_id=1, source_target_pairs={{20,0},{24,4},{28,8},{32,12},{36,16},{40,20},{44,24},{48,28},{52,3... | collective-permute-start | bytes 98312 | tf_op jit(solution)/shard_map/ppermute | solution.py:13
  124.6 20.4 %collective-permute-start.22 = (f32[2,16,256]{2,1,0:T(8,128)S(1)}, f32[2,16,256]{2,1,0:T(8,128)S(1)}, u32[]{:S(2)}, u32[]{:S(2)}) collective-permute-start(f32[2,16,256]{2,1,0:T(8,128)S(1)} %copy-done), channel_id=1, source_target_pairs={{24,0},{28,4},{32,8},{36,12},{40,16},{44,20},{48,24},{52,28},{56,3... | collective-permute-start | bytes 98312 | tf_op jit(solution)/shard_map/ppermute | solution.py:13
  132.0 21.1 %collective-permute-start.24 = (f32[2,16,256]{2,1,0:T(8,128)S(1)}, f32[2,16,256]{2,1,0:T(8,128)S(1)}, u32[]{:S(2)}, u32[]{:S(2)}) collective-permute-start(f32[2,16,256]{2,1,0:T(8,128)S(1)} %copy-done), channel_id=1, source_target_pairs={{32,0},{36,4},{40,8},{44,12},{48,16},{52,20},{56,24},{60,28},{64,3... | collective-permute-start | bytes 98312 | tf_op jit(solution)/shard_map/ppermute | solution.py:13
  135.9 21.6 %collective-permute-start.25 = (f32[2,16,256]{2,1,0:T(8,128)S(1)}, f32[2,16,256]{2,1,0:T(8,128)S(1)}, u32[]{:S(2)}, u32[]{:S(2)}) collective-permute-start(f32[2,16,256]{2,1,0:T(8,128)S(1)} %copy-done), channel_id=1, source_target_pairs={{36,0},{40,4},{44,8},{48,12},{52,16},{56,20},{60,24},{64,28},{68,3... | collective-permute-start | bytes 98312 | tf_op jit(solution)/shard_map/ppermute | solution.py:13
  153.1 22.1 %collective-permute-start.29 = (f32[2,16,256]{2,1,0:T(8,128)S(1)}, f32[2,16,256]{2,1,0:T(8,128)S(1)}, u32[]{:S(2)}, u32[]{:S(2)}) collective-permute-start(f32[2,16,256]{2,1,0:T(8,128)S(1)} %copy-done), channel_id=1, source_target_pairs={{52,0},{56,4},{60,8},{64,12},{68,16},{72,20},{76,24},{80,28},{84,3... | collective-permute-start | bytes 98312 | tf_op jit(solution)/shard_map/ppermute | solution.py:13
  163.8 24.5 %collective-permute-start.32 = (f32[2,16,256]{2,1,0:T(8,128)S(1)}, f32[2,16,256]{2,1,0:T(8,128)S(1)}, u32[]{:S(2)}, u32[]{:S(2)}) collective-permute-start(f32[2,16,256]{2,1,0:T(8,128)S(1)} %copy-done), channel_id=1, source_target_pairs={{64,0},{68,4},{72,8},{76,12},{80,16},{84,20},{88,24},{92,28},{96,3... | collective-permute-start | bytes 98312 | tf_op jit(solution)/shard_map/ppermute | solution.py:13
  165.7 24.5 %collective-permute-start.33 = (f32[2,16,256]{2,1,0:T(8,128)S(1)}, f32[2,16,256]{2,1,0:T(8,128)S(1)}, u32[]{:S(2)}, u32[]{:S(2)}) collective-permute-start(f32[2,16,256]{2,1,0:T(8,128)S(1)} %copy-done), channel_id=1, source_target_pairs={{68,0},{72,4},{76,8},{80,12},{84,16},{88,20},{92,24},{96,28},{100,... | collective-permute-start | bytes 98312 | tf_op jit(solution)/shard_map/ppermute | solution.py:13
  177.2 22.4 %collective-permute-start.73 = (f32[2,16,256]{2,1,0:T(8,128)S(1)}, f32[2,16,256]{2,1,0:T(8,128)S(1)}, u32[]{:S(2)}, u32[]{:S(2)}) collective-permute-start(f32[2,16,256]{2,1,0:T(8,128)S(1)} %copy-done.1), channel_id=1, source_target_pairs={{448,0},{452,4},{456,8},{460,12},{464,16},{468,20},{472,24},{476,2... | collective-permute-start | bytes 98312 | tf_op jit(solution)/shard_map/ppermute | solution.py:13
  179.5 23.8 %collective-permute-start.74 = (f32[2,16,256]{2,1,0:T(8,128)S(1)}, f32[2,16,256]{2,1,0:T(8,128)S(1)}, u32[]{:S(2)}, u32[]{:S(2)}) collective-permute-start(f32[2,16,256]{2,1,0:T(8,128)S(1)} %copy-done.1), channel_id=1, source_target_pairs={{452,0},{456,4},{460,8},{464,12},{468,16},{472,20},{476,24},{480,2... | collective-permute-start | bytes 98312 | tf_op jit(solution)/shard_map/ppermute | solution.py:13
  188.2 21.1 %collective-permute-start.75 = (f32[2,16,256]{2,1,0:T(8,128)S(1)}, f32[2,16,256]{2,1,0:T(8,128)S(1)}, u32[]{:S(2)}, u32[]{:S(2)}) collective-permute-start(f32[2,16,256]{2,1,0:T(8,128)S(1)} %copy-done.1), channel_id=1, source_target_pairs={{456,0},{460,4},{464,8},{468,12},{472,16},{476,20},{480,24},{484,2... | collective-permute-start | bytes 98312 | tf_op jit(solution)/shard_map/ppermute | solution.py:13
  190.2 21.1 %collective-permute-start.76 = (f32[2,16,256]{2,1,0:T(8,128)S(1)}, f32[2,16,256]{2,1,0:T(8,128)S(1)}, u32[]{:S(2)}, u32[]{:S(2)}) collective-permute-start(f32[2,16,256]{2,1,0:T(8,128)S(1)} %copy-done.1), channel_id=1, source_target_pairs={{460,0},{464,4},{468,8},{472,12},{476,16},{480,20},{484,24},{488,2... | collective-permute-start | bytes 98312 | tf_op jit(solution)/shard_map/ppermute | solution.py:13
  225.0 20.2 %collective-permute-start.85 = (f32[2,16,256]{2,1,0:T(8,128)S(1)}, f32[2,16,256]{2,1,0:T(8,128)S(1)}, u32[]{:S(2)}, u32[]{:S(2)}) collective-permute-start(f32[2,16,256]{2,1,0:T(8,128)S(1)} %copy-done.1), channel_id=1, source_target_pairs={{496,0},{500,4},{504,8},{508,12},{0,16},{4,20},{8,24},{12,28},{16,... | collective-permute-start | bytes 98312 | tf_op jit(solution)/shard_map/ppermute | solution.py:13
  254.0 21.6 %collective-permute-start.93 = (f32[2,16,256]{2,1,0:T(8,128)S(1)}, f32[2,16,256]{2,1,0:T(8,128)S(1)}, u32[]{:S(2)}, u32[]{:S(2)}) collective-permute-start(f32[2,16,256]{2,1,0:T(8,128)S(1)} %copy-done.1), channel_id=1, source_target_pairs={{20,0},{24,4},{28,8},{32,12},{36,16},{40,20},{44,24},{48,28},{52,3... | collective-permute-start | bytes 98312 | tf_op jit(solution)/shard_map/ppermute | solution.py:13
  257.1 20.4 %collective-permute-start.94 = (f32[2,16,256]{2,1,0:T(8,128)S(1)}, f32[2,16,256]{2,1,0:T(8,128)S(1)}, u32[]{:S(2)}, u32[]{:S(2)}) collective-permute-start(f32[2,16,256]{2,1,0:T(8,128)S(1)} %copy-done.1), channel_id=1, source_target_pairs={{24,0},{28,4},{32,8},{36,12},{40,16},{44,20},{48,24},{52,28},{56,3... | collective-permute-start | bytes 98312 | tf_op jit(solution)/shard_map/ppermute | solution.py:13
  264.8 21.0 %collective-permute-start.96 = (f32[2,16,256]{2,1,0:T(8,128)S(1)}, f32[2,16,256]{2,1,0:T(8,128)S(1)}, u32[]{:S(2)}, u32[]{:S(2)}) collective-permute-start(f32[2,16,256]{2,1,0:T(8,128)S(1)} %copy-done.1), channel_id=1, source_target_pairs={{32,0},{36,4},{40,8},{44,12},{48,16},{52,20},{56,24},{60,28},{64,3... | collective-permute-start | bytes 98312 | tf_op jit(solution)/shard_map/ppermute | solution.py:13
  269.3 21.6 %collective-permute-start.97 = (f32[2,16,256]{2,1,0:T(8,128)S(1)}, f32[2,16,256]{2,1,0:T(8,128)S(1)}, u32[]{:S(2)}, u32[]{:S(2)}) collective-permute-start(f32[2,16,256]{2,1,0:T(8,128)S(1)} %copy-done.1), channel_id=1, source_target_pairs={{36,0},{40,4},{44,8},{48,12},{52,16},{56,20},{60,24},{64,28},{68,3... | collective-permute-start | bytes 98312 | tf_op jit(solution)/shard_map/ppermute | solution.py:13
  285.8 22.9 %collective-permute-start.101 = (f32[2,16,256]{2,1,0:T(8,128)S(1)}, f32[2,16,256]{2,1,0:T(8,128)S(1)}, u32[]{:S(2)}, u32[]{:S(2)}) collective-permute-start(f32[2,16,256]{2,1,0:T(8,128)S(1)} %copy-done.1), channel_id=1, source_target_pairs={{52,0},{56,4},{60,8},{64,12},{68,16},{72,20},{76,24},{80,28},{84,3... | collective-permute-start | bytes 98312 | tf_op jit(solution)/shard_map/ppermute | solution.py:13
  290.9 41.9 %collective-permute-start.102 = (f32[2,16,256]{2,1,0:T(8,128)S(1)}, f32[2,16,256]{2,1,0:T(8,128)S(1)}, u32[]{:S(2)}, u32[]{:S(2)}) collective-permute-start(f32[2,16,256]{2,1,0:T(8,128)S(1)} %copy-done.1), channel_id=1, source_target_pairs={{56,0},{60,4},{64,8},{68,12},{72,16},{76,20},{80,24},{84,28},{88,3... | collective-permute-start | bytes 98312 | tf_op jit(solution)/shard_map/ppermute | solution.py:13
  295.7 39.1 %collective-permute-start.103 = (f32[2,16,256]{2,1,0:T(8,128)S(1)}, f32[2,16,256]{2,1,0:T(8,128)S(1)}, u32[]{:S(2)}, u32[]{:S(2)}) collective-permute-start(f32[2,16,256]{2,1,0:T(8,128)S(1)} %copy-done.1), channel_id=1, source_target_pairs={{60,0},{64,4},{68,8},{72,12},{76,16},{80,20},{84,24},{88,28},{92,3... | collective-permute-start | bytes 98312 | tf_op jit(solution)/shard_map/ppermute | solution.py:13
  297.6 37.2 %collective-permute-start.104 = (f32[2,16,256]{2,1,0:T(8,128)S(1)}, f32[2,16,256]{2,1,0:T(8,128)S(1)}, u32[]{:S(2)}, u32[]{:S(2)}) collective-permute-start(f32[2,16,256]{2,1,0:T(8,128)S(1)} %copy-done.1), channel_id=1, source_target_pairs={{64,0},{68,4},{72,8},{76,12},{80,16},{84,20},{88,24},{92,28},{96,3... | collective-permute-start | bytes 98312 | tf_op jit(solution)/shard_map/ppermute | solution.py:13
  299.6 35.3 %collective-permute-start.105 = (f32[2,16,256]{2,1,0:T(8,128)S(1)}, f32[2,16,256]{2,1,0:T(8,128)S(1)}, u32[]{:S(2)}, u32[]{:S(2)}) collective-permute-start(f32[2,16,256]{2,1,0:T(8,128)S(1)} %copy-done.1), channel_id=1, source_target_pairs={{68,0},{72,4},{76,8},{80,12},{84,16},{88,20},{92,24},{96,28},{100,... | collective-permute-start | bytes 98312 | tf_op jit(solution)/shard_map/ppermute | solution.py:13
  308.7 38.2 %collective-permute-start.34 = (f32[2,16,34]{2,1,0:T(8,128)S(1)}, f32[2,16,34]{2,1,0:T(8,128)S(1)}, u32[]{:S(2)}, u32[]{:S(2)}) collective-permute-start(f32[2,16,34]{2,1,0:T(8,128)S(1)} %slice.271), channel_id=1, source_target_pairs={{0,1},{1,2},{2,3},{3,0},{4,5},{5,6},{6,7},{7,4},{8,9},{9,10},{10,1... | collective-permute-start | bytes 13064 | tf_op jit(solution)/shard_map/ppermute | solution.py:23
  335.0 187.3 %collective-permute-start.106 = (f32[2,16,34]{2,1,0:T(8,128)S(1)}, f32[2,16,34]{2,1,0:T(8,128)S(1)}, u32[]{:S(2)}, u32[]{:S(2)}) collective-permute-start(f32[2,16,34]{2,1,0:T(8,128)S(1)} %slice.287), channel_id=1, source_target_pairs={{0,1},{1,2},{2,3},{3,0},{4,5},{5,6},{6,7},{7,4},{8,9},{9,10},{10,1... | collective-permute-start | bytes 13064 | tf_op jit(solution)/shard_map/ppermute | solution.py:23
  347.2 33.8 %collective-permute-start.36 = (f32[2,16,256]{2,1,0:T(8,128)S(1)}, f32[2,16,256]{2,1,0:T(8,128)S(1)}, u32[]{:S(2)}, u32[]{:S(2)}) collective-permute-start(f32[2,16,256]{2,1,0:T(8,128)S(1)} %fusion.7), channel_id=1, source_target_pairs={{444,0},{448,4},{452,8},{456,12},{460,16},{464,20},{468,24},{472,2... | collective-permute-start | bytes 98312 | tf_op jit(solution)/shard_map/ppermute | solution.py:13
  352.7 169.6 %collective-permute-start.107 = (f32[2,16,34]{2,1,0:T(8,128)S(1)}, f32[2,16,34]{2,1,0:T(8,128)S(1)}, u32[]{:S(2)}, u32[]{:S(2)}) collective-permute-start(f32[2,16,34]{2,1,0:T(8,128)S(1)} %bitcast.45), channel_id=1, source_target_pairs={{1,0},{2,1},{3,2},{0,3},{5,4},{6,5},{7,6},{4,7},{9,8},{10,9},{11,1... | collective-permute-start | bytes 13064 | tf_op jit(solution)/shard_map/ppermute | solution.py:25
  (78 other events, 1367.7 us)
where the time goes:
time: 531 us; the launch traced here: 528 us
  starting transfers between devices  481 us (91%)
  between operations  30.6 us (6%)
  waiting for transfers between devices  7.44 us (1%)
  local copies, waits for them, and re-layouts  6.13 us (1%)
    ppermute x102, starting transfers between devices, shifted(): return lax.ppermute(block, axis, route)  409 us
    ppermute x3, starting transfers between devices, padded(): lax.ppermute(tail, axis, [(i, (i + 1) % count) for i in range(count)])  50.4 us
    ppermute x3, starting transfers between devices, padded(): lax.ppermute(head, axis, [((i + 1) % count, i) for i in range(count)])  21 us
  transfers between devices with their start and end apart: 108, of which 4 were waited for; matrix products, arithmetic and copies ran while one was open for 2% of the time, Pallas kernels for 0%

commit v1 on v0

v1 whole, which is shorter than its diff:
```python
import jax
import jax.numpy as jnp
from jax import lax
from jax.experimental import pallas as pl
from jax.experimental.pallas import tpu as pltpu
from jax.sharding import PartitionSpec as P

MESH = pl.DeviceIdType.MESH
PLANES = 16
GROUP = 8
RING = 4
HALF = 64
OWN = 17
WINDOW = 42


def cubic_weights(fraction):
    position = 1.0 - jnp.full((8, 128), fraction, jnp.float32)
    taps = (
        -position * (position - 1.0) * (position - 2.0) / 6.0,
        (position + 1.0) * (position - 1.0) * (position - 2.0) / 2.0,
        -(position + 1.0) * position * (position - 2.0) / 2.0,
        (position + 1.0) * position * (position - 1.0) / 6.0,
    )
    return taps[::-1]


def kernel(
    fine_hbm,
    coarse_hbm,
    upstream_x_hbm,
    upstream_y_hbm,
    fractions_hbm,
    out_ref,
    fine_ref,
    coarse_ref,
    upstream_x,
    upstream_y,
    fractions,
    packed_f,
    packed_c,
    window_1,
    window_0,
    window_2,
    rows,
    beside,
    swept_0,
    swept_2,
    back_f,
    back_c,
    sent,
    got,
    brought,
):
    arrivals = [
        pltpu.make_async_copy(source, target, brought.at[i])
        for i, (source, target) in enumerate(
            (
                (fine_hbm, fine_ref),
                (upstream_x_hbm, upstream_x),
                (upstream_y_hbm, upstream_y),
                (fractions_hbm, fractions),
                (coarse_hbm, coarse_ref),
            )
        )
    ]
    for arrival in arrivals:
        arrival.start()
    gx, gy = lax.axis_index("gx"), lax.axis_index("gy")
    plane, member = gx // GROUP, lax.rem(gx, GROUP)
    quarter, level = lax.rem(member, 4), member // 4
    lane = lax.broadcasted_iota(jnp.int32, (8, 128), 1)
    low = lane < HALF
    within = lax.rem(lane, HALF)

    def in_plane(other, gy_step=0):
        return plane * GROUP + other, lax.rem(gy + gy_step + RING, RING)

    def up_planes(step):
        return lax.rem(plane + step + PLANES, PLANES) * GROUP + member, gy

    def mate(step):
        return lax.rem(member + step, GROUP)

    def swap(tile):
        return pltpu.roll(tile, HALF, 1)

    def remote(source, target, channel, device, leave=None):
        leave = channel if leave is None else leave
        return pltpu.make_async_remote_copy(
            source, target, sent.at[leave], got.at[channel], device_id=device, device_id_type=MESH
        )

    def drain(ref, semaphores, channel):
        pltpu.make_async_copy(ref, ref, semaphores.at[channel]).wait()

    barrier = pltpu.get_barrier_semaphore()

    def greet(device):
        pl.semaphore_signal(barrier, inc=1, device_id=device, device_id_type=MESH)

    for step in (3, -3, 2, -2, 1, -1):
        greet(up_planes(step))
    for half in range(2):
        greet(in_plane(4 * half, 1))
        greet(in_plane(4 * half + 3, -1))
    for step in range(1, GROUP):
        greet(in_plane(mate(step)))
    edge = jnp.logical_or(quarter == 0, quarter == 3)

    def pack(field, packed):
        for lev in range(2):
            for block in range(2):
                columns = slice(128 * block, 128 * block + 128)
                upper = field[lev, 0:8, columns]
                lower = field[lev, 8:16, columns]
                packed[lev * 4 + 2 * block] = jnp.where(low, upper, swap(lower))
                packed[lev * 4 + 2 * block + 1] = jnp.where(low, swap(upper), lower)

    def transpose_start(packed, window, channel):
        for step in range(1, GROUP):
            other = mate(step)
            remote(packed.at[other], window.at[OWN + member], channel, in_plane(other)).start()
        window[OWN + member] = packed[member]

    def transpose_wait(window, channel):
        drain(window.at[pl.ds(0, 7)], got, channel)

    def planes_start(window, channel):
        own = window.at[pl.ds(OWN, 8)]
        remote(window.at[OWN + 7], window.at[0], channel, up_planes(3)).start()
        remote(window.at[OWN], window.at[WINDOW - 1], channel, up_planes(-3)).start()
        for step in (2, -2, 1, -1):
            remote(own, window.at[pl.ds(OWN - 8 * step, 8)], channel, up_planes(step)).start()

    def planes_wait(window, channel):
        drain(window.at[pl.ds(0, 34)], got, channel)

    def sweep_x(window, pass_row, target):
        shift = upstream_x[pass_row, 2 * gy + quarter // 2]
        weights = cubic_weights(fractions[0, pass_row])
        start = shift - 1 + 16 * OWN
        first, odd, inner = start // 16, lax.rem(start // 8, 2), lax.rem(start, 8)
        even_tiles = [window[first + i] for i in range(10)]
        swapped = [swap(tile) for tile in even_tiles]
        odd_tiles = [jnp.where(low, swapped[i], swapped[i + 1]) for i in range(9)]
        is_odd = jnp.full((8, 128), odd, jnp.int32) == 1
        lead = [jnp.where(is_odd, odd_tiles[i], even_tiles[i]) for i in range(9)]
        for i in range(8):
            rows[i, 0:8] = lead[i]
            rows[i, 8:16] = jnp.where(is_odd, even_tiles[i + 1], odd_tiles[i])
            rows[i, 16:24] = lead[i + 1]
        for i in range(8):
            summed = weights[0] * rows[i, pl.ds(inner, 8)]
            for tap in range(1, 4):
                summed = summed + weights[tap] * rows[i, pl.ds(inner + tap, 8)]
            target(i, summed)

    def sweep_y(pass_row, load, count):
        shift = upstream_y[pass_row, plane]
        weights = cubic_weights(fractions[1, pass_row])
        sums = [None] * count
        for tap in range(4):
            offset = shift - 1 + tap
            side = (offset >= 0).astype(jnp.int32)
            turn = offset + HALF * (1 - side)
            here = within + turn < HALF
            for i in range(count):
                cells = jnp.where(
                    here,
                    pltpu.roll(load(i, side), lax.rem(128 - turn, 128), 1),
                    pltpu.roll(load(i, side + 1), HALF - turn, 1),
                )
                term = weights[tap] * cells
                sums[i] = term if sums[i] is None else sums[i] + term
        return sums

    def back_start(swept, back, channel):
        for step in range(1, GROUP):
            other = mate(step)
            remote(swept.at[other], back.at[level, quarter + 1], channel, in_plane(other)).start()
        back[level, quarter + 1] = swept[member]

        @pl.when(edge)
        def _():
            side = jnp.where(quarter == 0, 5, 0)
            gy_step = jnp.where(quarter == 0, -1, 1)
            for other in range(GROUP):
                remote(swept.at[other], back.at[level, side], channel, in_plane(other, gy_step), channel + 2).start()

    def back_wait(channel):
        drain(window_0.at[pl.ds(0, 11)], got, channel)

    arrivals[0].wait()
    pack(fine_ref, packed_f)
    pl.semaphore_wait(barrier, jnp.where(edge, 21, 13))
    transpose_start(packed_f, window_1, 0)
    arrivals[4].wait()
    pack(coarse_ref, packed_c)
    transpose_start(packed_c, window_2, 1)
    for arrival in arrivals[1:4]:
        arrival.wait()
    transpose_wait(window_1, 0)
    planes_start(window_1, 2)
    planes_wait(window_1, 2)

    def keep_1(i, tile):
        beside[1, i] = tile

    sweep_x(window_1, 1, keep_1)
    right = jnp.where(quarter == 3, member - 3, member + 1)
    left = jnp.where(quarter == 0, member + 3, member - 1)
    remote(beside.at[1], beside.at[0], 3, in_plane(right, (quarter == 3).astype(jnp.int32))).start()
    remote(beside.at[1], beside.at[2], 3, in_plane(left, -(quarter == 0).astype(jnp.int32))).start()
    transpose_wait(window_2, 1)
    planes_start(window_2, 4)
    drain(window_1.at[pl.ds(0, 16)], got, 3)

    for i, tile in enumerate(sweep_y(1, lambda i, side: beside[side, i], 8)):
        window_0[OWN + i] = tile
    planes_start(window_0, 5)

    def keep_2(i, tile):
        swept_2[i] = tile

    planes_wait(window_2, 4)
    sweep_x(window_2, 2, keep_2)
    back_start(swept_2, back_c, 6)

    def keep_0(i, tile):
        swept_0[i] = tile

    planes_wait(window_0, 5)
    sweep_x(window_0, 0, keep_0)
    back_start(swept_0, back_f, 7)

    back_wait(6)
    coarse = sweep_y(2, lambda i, side: back_c[i // 4, lax.rem(i, 4) + side], 8)
    back_wait(7)
    fine = sweep_y(0, lambda i, side: back_f[i // 4, lax.rem(i, 4) + side], 8)
    tiles = [a - b for a, b in zip(fine, coarse)]
    for lev in range(2):
        for block in range(2):
            columns = slice(128 * block, 128 * block + 128)
            even, odd = tiles[lev * 4 + 2 * block], tiles[lev * 4 + 2 * block + 1]
            out_ref[lev, 0:8, columns] = jnp.where(low, even, swap(odd))
            out_ref[lev, 8:16, columns] = jnp.where(low, swap(even), odd)

    for channel in (0, 1):
        drain(window_0.at[pl.ds(0, 7)], sent, channel)
    for channel in (2, 4, 5):
        drain(window_0.at[pl.ds(0, 34)], sent, channel)
    drain(window_0.at[pl.ds(0, 16)], sent, 3)
    for channel in (6, 7):
        drain(window_0.at[pl.ds(0, 7)], sent, channel)

        @pl.when(edge)
        def _():
            drain(window_0.at[pl.ds(0, 8)], sent, channel + 2)


def local(fine_cotangent, coarse_cotangent, upstream_x, upstream_y, fractions):
    vmem = pl.BlockSpec(memory_space=pltpu.VMEM)
    anywhere = pl.BlockSpec(memory_space=pl.ANY)

    def tiles(*shape):
        return pltpu.VMEM((*shape, 8, 128), jnp.float32)

    return pl.pallas_call(
        kernel,
        out_shape=pltpu.VMEM(fine_cotangent.shape, jnp.float32),
        in_specs=[anywhere] * 5,
        out_specs=vmem,
        scratch_shapes=[
            pltpu.VMEM(fine_cotangent.shape, jnp.float32),
            pltpu.VMEM(fine_cotangent.shape, jnp.float32),
            pltpu.SMEM(upstream_x.shape, jnp.int32),
            pltpu.SMEM(upstream_y.shape, jnp.int32),
            pltpu.SMEM((2, 3), jnp.float32),
            tiles(GROUP),
            tiles(GROUP),
            tiles(WINDOW),
            tiles(WINDOW),
            tiles(WINDOW),
            pltpu.VMEM((8, 24, 128), jnp.float32),
            tiles(3, 8),
            tiles(8),
            tiles(8),
            tiles(2, 6),
            tiles(2, 6),
            pltpu.SemaphoreType.DMA((10,)),
            pltpu.SemaphoreType.DMA((8,)),
            pltpu.SemaphoreType.DMA((5,)),
        ],
        compiler_params=pltpu.CompilerParams(collective_id=0, has_side_effects=True),
    )(fine_cotangent, coarse_cotangent, upstream_x, upstream_y, fractions.T)


def solution(mesh):
    placed = (P(None, "gx", "gy"), P(None, "gx", "gy"), P(), P(), P())
    return jax.shard_map(
        local, mesh=mesh, in_specs=placed, out_specs=P(None, "gx", "gy"), check_vma=False
    )
```

time: 531 us -> 36.1 us (0.07)
  starting transfers between devices: 481 us -> 0 us
  Pallas kernels: 0 us -> 35.3 us
  between operations: 30.6 us -> 0.01 us
  waiting for transfers between devices: 7.44 us -> 0 us
  local copies, waits for them, and re-layouts: 6.13 us -> 0.62 us
    ppermute x108 -> x0, starting transfers between devices: 481 us -> none  [the longest x102 409 us: shifted(): return lax.ppermute(block, axis, route)]
    pallas_call x0 -> x1, Pallas kernels: none -> 35.3 us  [local(): pl.pallas_call(kernel, out_shape=pltpu.VMEM(fine_cotangent.shape, jnp.flo...]
    ppermute x108 -> x0, waiting for transfers between devices: 7.44 us -> none  [the longest x3 4.48 us: padded(): lax.ppermute(head, axis, [((i + 1) % count, i) for i in range(count)])]
    slice x12 -> x0, local copies, waits for them, and re-layouts: 5.43 us -> none  [the longest x3 1.83 us: sweep_x(): local_shifts[block_index]]
  transfers between devices with their start and end apart: 108 -> 0, of which waited for: 4 -> 0; matrix products, arithmetic and copies ran while one was open for 2% -> 0% of each run, Pallas kernels for 0% -> 0%
where the time goes in v1:
time: 36.1 us; the launch traced here: 35.9 us
  Pallas kernels  35.3 us (98%)
  local copies, waits for them, and re-layouts  0.62 us (2%)
    pallas_call x1, Pallas kernels, local(): pl.pallas_call(kernel, out_shape=pltpu.VMEM(fine_cotangent.shape, jnp.flo...  35.3 us

profile of v1, /device:TPU:1, one launch (start us, length us, event | category | flops | bytes accessed | tf_op | source)
XLA Modules:
  0.0 35.9 jit_solution(17840806969794189788)
XLA Ops:
  0.0 35.3 %shard_map.55 = f32[2,16,256]{2,1,0:T(8,128)S(1)} custom-call(f32[2,16,256]{2,1,0:T(8,128)} %fine_hbm.1, f32[2,16,256]{2,1,0:T(8,128)} %coarse_hbm.1, s32[3,8]{1,0:T(4,128)} %upstream_x_hbm.1, s32[3,16]{1,0:T(4,128)} %upstream_y_hbm.1, f32[2,3]{1,0:T(2,128)} %bitcast.1), custom_call_target="tpu_custom_call" | custom-call | tf_op jit(solution)/shard_map/pallas_call | solution.py:269
  35.3 0.6 %copy.7 = f32[2,16,256]{2,1,0:T(8,128)} copy(f32[2,16,256]{2,1,0:T(8,128)S(1)} %shard_map.55) | data formatting | bytes 65536

commit v2 on v1

--- a/solution.py
+++ b/solution.py
@@ -39,11 +39,14 @@
     fractions,
     packed_f,
     packed_c,
+    cells,
+    edges,
+    ahead,
+    fringe,
     window_1,
     window_0,
     window_2,
     rows,
-    beside,
     swept_0,
     swept_2,
     back_f,
@@ -99,23 +102,27 @@
     def greet(device):
         pl.semaphore_signal(barrier, inc=1, device_id=device, device_id_type=MESH)
 
+    edge = jnp.logical_or(quarter == 0, quarter == 3)
+    outward = jnp.where(quarter == 0, -1, 1)
     for step in (3, -3, 2, -2, 1, -1):
         greet(up_planes(step))
-    for half in range(2):
-        greet(in_plane(4 * half, 1))
-        greet(in_plane(4 * half + 3, -1))
+
+    @pl.when(edge)
+    def _():
+        for other in range(GROUP):
+            greet(in_plane(other, outward))
+
     for step in range(1, GROUP):
         greet(in_plane(mate(step)))
-    edge = jnp.logical_or(quarter == 0, quarter == 3)
-
-    def pack(field, packed):
+
+    def pack(field, place):
         for lev in range(2):
             for block in range(2):
                 columns = slice(128 * block, 128 * block + 128)
                 upper = field[lev, 0:8, columns]
                 lower = field[lev, 8:16, columns]
-                packed[lev * 4 + 2 * block] = jnp.where(low, upper, swap(lower))
-                packed[lev * 4 + 2 * block + 1] = jnp.where(low, swap(upper), lower)
+                place(lev, 2 * block, jnp.where(low, upper, swap(lower)))
+                place(lev, 2 * block + 1, jnp.where(low, swap(upper), lower))
 
     def transpose_start(packed, window, channel):
         for step in range(1, GROUP):
@@ -136,12 +143,12 @@
     def planes_wait(window, channel):
         drain(window.at[pl.ds(0, 34)], got, channel)
 
-    def sweep_x(window, pass_row, target):
-        shift = upstream_x[pass_row, 2 * gy + quarter // 2]
+    def sweep_x(load, pass_row, block):
+        shift = upstream_x[pass_row, block]
         weights = cubic_weights(fractions[0, pass_row])
         start = shift - 1 + 16 * OWN
         first, odd, inner = start // 16, lax.rem(start // 8, 2), lax.rem(start, 8)
-        even_tiles = [window[first + i] for i in range(10)]
+        even_tiles = [load(first + i) for i in range(10)]
         swapped = [swap(tile) for tile in even_tiles]
         odd_tiles = [jnp.where(low, swapped[i], swapped[i + 1]) for i in range(9)]
         is_odd = jnp.full((8, 128), odd, jnp.int32) == 1
@@ -150,28 +157,77 @@
             rows[i, 0:8] = lead[i]
             rows[i, 8:16] = jnp.where(is_odd, even_tiles[i + 1], odd_tiles[i])
             rows[i, 16:24] = lead[i + 1]
+        sums = []
         for i in range(8):
             summed = weights[0] * rows[i, pl.ds(inner, 8)]
             for tap in range(1, 4):
                 summed = summed + weights[tap] * rows[i, pl.ds(inner + tap, 8)]
-            target(i, summed)
+            sums.append(summed)
+        return sums
+
+    def shifted_cells(load, i, offset):
+        side = (offset >= 0).astype(jnp.int32)
+        turn = offset + HALF * (1 - side)
+        return jnp.where(
+            within + turn < HALF,
+            pltpu.roll(load(i, side), lax.rem(128 - turn, 128), 1),
+            pltpu.roll(load(i, side + 1), HALF - turn, 1),
+        )
+
+    border = HALF * lax.rem(quarter, 2)
+    low_block = lax.rem(2 * gy + (quarter + 1) // 2 - 1 + 2 * RING, 2 * RING)
+    high_block = lax.rem(low_block + 1, 2 * RING)
+
+    def crossing_of(to_plane):
+        return border - upstream_y[1, to_plane] - 2
+
+    def sweep_y_ahead(to_plane, tiles, target, at):
+        shift = upstream_y[1, to_plane]
+        crossing = crossing_of(to_plane)
+        upper_columns = within > crossing + 2
+        spare = jnp.zeros((8, 128), jnp.float32)
+        parts = []
+        for tap, weight in enumerate(cubic_weights(fractions[1, 1])):
+            offset = shift - 1 + tap
+            split = jnp.logical_and(within + offset >= border, jnp.logical_not(upper_columns))
+            parts.append((offset, jnp.where(split, 0.0, weight), jnp.where(split, weight, 0.0)))
+        for n, i in enumerate(tiles):
+            main = jnp.zeros((8, 128), jnp.float32)
+            second = jnp.zeros((8, 128), jnp.float32)
+            for offset, first_weight, second_weight in parts:
+                moved = shifted_cells(lambda i, side: cells[i, side], i, offset)
+                main = main + first_weight * moved
+                second = second + second_weight * moved
+            target[at + n] = main
+            spare = spare + pltpu.roll(second, lax.rem(8 * i - crossing + 256, 128), 1)
+        target[at + len(tiles)] = spare
+
+    def sweep_x_both():
+        crossing = crossing_of(plane)
+        upper_columns = within > crossing + 2
+        both = jnp.logical_and(within >= crossing, within <= crossing + 2)
+
+        def load_low(i):
+            place = 9 * ((i + 7) // 8) + lax.rem(i + 7, 8)
+            return jnp.where(upper_columns, 0.0, window_1[place])
+
+        def load_high(i):
+            level_plane, inside = (i + 7) // 8, lax.rem(i + 7, 8)
+            spare = window_1[jnp.where(level_plane == 6, 55, 9 * level_plane + 8)]
+            spare = pltpu.roll(spare, lax.rem(crossing - 8 * inside + 256, 128), 1)
+            return jnp.where(upper_columns, window_1[9 * level_plane + inside], jnp.where(both, spare, 0.0))
+
+        low_part = sweep_x(load_low, 1, low_block)
+        high_part = sweep_x(load_high, 1, high_block)
+        return [a + b for a, b in zip(low_part, high_part)]
 
     def sweep_y(pass_row, load, count):
         shift = upstream_y[pass_row, plane]
         weights = cubic_weights(fractions[1, pass_row])
         sums = [None] * count
         for tap in range(4):
-            offset = shift - 1 + tap
-            side = (offset >= 0).astype(jnp.int32)
-            turn = offset + HALF * (1 - side)
-            here = within + turn < HALF
             for i in range(count):
-                cells = jnp.where(
-                    here,
-                    pltpu.roll(load(i, side), lax.rem(128 - turn, 128), 1),
-                    pltpu.roll(load(i, side + 1), HALF - turn, 1),
-                )
-                term = weights[tap] * cells
+                term = weights[tap] * shifted_cells(load, i, shift - 1 + tap)
                 sums[i] = term if sums[i] is None else sums[i] + term
         return sums
 
@@ -184,54 +240,76 @@
         @pl.when(edge)
         def _():
             side = jnp.where(quarter == 0, 5, 0)
-            gy_step = jnp.where(quarter == 0, -1, 1)
             for other in range(GROUP):
-                remote(swept.at[other], back.at[level, side], channel, in_plane(other, gy_step), channel + 2).start()
+                remote(swept.at[other], back.at[level, side], channel, in_plane(other, outward), channel + 2).start()
 
     def back_wait(channel):
         drain(window_0.at[pl.ds(0, 11)], got, channel)
 
+    def place_f(lev, part, tile):
+        packed_f[lev, part + 1] = tile
+
+    def place_c(lev, part, tile):
+        packed_c[4 * lev + part] = tile
+
+    for lev in range(2):
+        packed_f[lev, 0] = jnp.zeros((8, 128), jnp.float32)
+        packed_f[lev, 5] = jnp.zeros((8, 128), jnp.float32)
     arrivals[0].wait()
-    pack(fine_ref, packed_f)
-    pl.semaphore_wait(barrier, jnp.where(edge, 21, 13))
-    transpose_start(packed_f, window_1, 0)
+    pack(fine_ref, place_f)
+    pl.semaphore_wait(barrier, 17)
+
+    for lev in range(2):
+        remote(packed_f.at[lev, 4], edges.at[member], 3, in_plane(4 * lev, 1)).start()
+        remote(packed_f.at[lev, 1], edges.at[member], 3, in_plane(4 * lev + 3, -1)).start()
+    for step in range(1, GROUP):
+        other = mate(step)
+        source = packed_f.at[other // 4, pl.ds(lax.rem(other, 4), 3)]
+        remote(source, cells.at[member], 0, in_plane(other)).start()
+    cells[member] = packed_f[level, pl.ds(quarter, 3)]
     arrivals[4].wait()
-    pack(coarse_ref, packed_c)
+    pack(coarse_ref, place_c)
     transpose_start(packed_c, window_2, 1)
     for arrival in arrivals[1:4]:
         arrival.wait()
-    transpose_wait(window_1, 0)
-    planes_start(window_1, 2)
-    planes_wait(window_1, 2)
-
-    def keep_1(i, tile):
-        beside[1, i] = tile
-
-    sweep_x(window_1, 1, keep_1)
-    right = jnp.where(quarter == 3, member - 3, member + 1)
-    left = jnp.where(quarter == 0, member + 3, member - 1)
-    remote(beside.at[1], beside.at[0], 3, in_plane(right, (quarter == 3).astype(jnp.int32))).start()
-    remote(beside.at[1], beside.at[2], 3, in_plane(left, -(quarter == 0).astype(jnp.int32))).start()
+    drain(cells.at[pl.ds(0, 7)], got, 0)
+
+    @pl.when(edge)
+    def _():
+        drain(edges, got, 3)
+        side = jnp.where(quarter == 0, 0, 2)
+        for i in range(8):
+            cells[i, side] = edges[i]
+
+    def to(step):
+        return lax.rem(plane + step + PLANES, PLANES)
+
+    sweep_y_ahead(to(3), (7,), fringe, 0)
+    remote(fringe.at[pl.ds(0, 2)], window_1.at[pl.ds(7, 2)], 2, up_planes(3)).start()
+    sweep_y_ahead(to(-3), (0,), fringe, 2)
+    remote(fringe.at[pl.ds(2, 2)], window_1.at[pl.ds(54, 2)], 2, up_planes(-3)).start()
+    for n, step in enumerate((2, -2, 1, -1)):
+        sweep_y_ahead(to(step), range(8), ahead, 9 * n)
+        target = window_1.at[pl.ds(9 * (3 - step), 9)]
+        remote(ahead.at[pl.ds(9 * n, 9)], target, 2, up_planes(step)).start()
+    sweep_y_ahead(plane, range(8), window_1, 27)
     transpose_wait(window_2, 1)
     planes_start(window_2, 4)
-    drain(window_1.at[pl.ds(0, 16)], got, 3)
-
-    for i, tile in enumerate(sweep_y(1, lambda i, side: beside[side, i], 8)):
+    drain(window_1.at[pl.ds(0, 40)], got, 2)
+
+    for i, tile in enumerate(sweep_x_both()):
         window_0[OWN + i] = tile
     planes_start(window_0, 5)
 
-    def keep_2(i, tile):
+    own_block = 2 * gy + quarter // 2
+    planes_wait(window_2, 4)
+    for i, tile in enumerate(sweep_x(lambda i: window_2[i], 2, own_block)):
         swept_2[i] = tile
-
-    planes_wait(window_2, 4)
-    sweep_x(window_2, 2, keep_2)
     back_start(swept_2, back_c, 6)
 
-    def keep_0(i, tile):
+    planes_wait(window_0, 5)
+    for i, tile in enumerate(sweep_x(lambda i: window_0[i], 0, own_block)):
         swept_0[i] = tile
-
-    planes_wait(window_0, 5)
-    sweep_x(window_0, 0, keep_0)
     back_start(swept_0, back_f, 7)
 
     back_wait(6)
@@ -246,11 +324,12 @@
             out_ref[lev, 0:8, columns] = jnp.where(low, even, swap(odd))
             out_ref[lev, 8:16, columns] = jnp.where(low, swap(even), odd)
 
-    for channel in (0, 1):
-        drain(window_0.at[pl.ds(0, 7)], sent, channel)
-    for channel in (2, 4, 5):
+    drain(cells.at[pl.ds(0, 7)], sent, 0)
+    drain(window_0.at[pl.ds(0, 7)], sent, 1)
+    drain(window_0.at[pl.ds(0, 4)], sent, 3)
+    drain(window_1.at[pl.ds(0, 40)], sent, 2)
+    for channel in (4, 5):
         drain(window_0.at[pl.ds(0, 34)], sent, channel)
-    drain(window_0.at[pl.ds(0, 16)], sent, 3)
     for channel in (6, 7):
         drain(window_0.at[pl.ds(0, 7)], sent, channel)
 
@@ -277,13 +356,16 @@
             pltpu.SMEM(upstream_x.shape, jnp.int32),
             pltpu.SMEM(upstream_y.shape, jnp.int32),
             pltpu.SMEM((2, 3), jnp.float32),
+            tiles(2, 6),
             tiles(GROUP),
-            tiles(GROUP),
-            tiles(WINDOW),
+            tiles(8, 3),
+            tiles(8),
+            tiles(36),
+            tiles(4),
+            tiles(63),
             tiles(WINDOW),
             tiles(WINDOW),
             pltpu.VMEM((8, 24, 128), jnp.float32),
-            tiles(3, 8),
             tiles(8),
             tiles(8),
             tiles(2, 6),

time: 36.1 us -> 34.9 us (0.967)
  Pallas kernels: 35.3 us -> 34.1 us
    pallas_call x1, Pallas kernels: 35.3 us -> 34.1 us  [local(): pl.pallas_call(kernel, out_shape=pltpu.VMEM(fine_cotangent.shape, jnp.flo...]
where the time goes in v2:
time: 34.9 us; the launch traced here: 34.7 us
  Pallas kernels  34.1 us (98%)
  local copies, waits for them, and re-layouts  0.62 us (2%)
    pallas_call x1, Pallas kernels, local(): pl.pallas_call(kernel, out_shape=pltpu.VMEM(fine_cotangent.shape, jnp.flo...  34.1 us

profile of v2, /device:TPU:1, one launch (start us, length us, event | category | flops | bytes accessed | tf_op | source)
XLA Modules:
  0.0 34.7 jit_solution(16821862154882129862)
XLA Ops:
  0.0 34.1 %shard_map.55 = f32[2,16,256]{2,1,0:T(8,128)S(1)} custom-call(f32[2,16,256]{2,1,0:T(8,128)} %fine_hbm.1, f32[2,16,256]{2,1,0:T(8,128)} %coarse_hbm.1, s32[3,8]{1,0:T(4,128)} %upstream_x_hbm.1, s32[3,16]{1,0:T(4,128)} %upstream_y_hbm.1, f32[2,3]{1,0:T(2,128)} %bitcast.1), custom_call_target="tpu_custom_call" | custom-call | tf_op jit(solution)/shard_map/pallas_call | solution.py:348
  34.1 0.6 %copy.7 = f32[2,16,256]{2,1,0:T(8,128)} copy(f32[2,16,256]{2,1,0:T(8,128)S(1)} %shard_map.55) | data formatting | bytes 65536

commit v3 on v2

--- a/solution.py
+++ b/solution.py
@@ -44,10 +44,11 @@
     ahead,
     fringe,
     window_1,
-    window_0,
+    ready,
+    strewn,
+    swept_0,
     window_2,
     rows,
-    swept_0,
     swept_2,
     back_f,
     back_c,
@@ -147,18 +148,22 @@
         shift = upstream_x[pass_row, block]
         weights = cubic_weights(fractions[0, pass_row])
         start = shift - 1 + 16 * OWN
-        first, odd, inner = start // 16, lax.rem(start // 8, 2), lax.rem(start, 8)
-        even_tiles = [load(first + i) for i in range(10)]
+        first = start // 16
+        return slide([load(first + i) for i in range(10)], start, weights)
+
+    def slide(even_tiles, start, weights):
+        count = len(even_tiles) - 2
+        odd, inner = lax.rem(start // 8, 2), lax.rem(start, 8)
         swapped = [swap(tile) for tile in even_tiles]
-        odd_tiles = [jnp.where(low, swapped[i], swapped[i + 1]) for i in range(9)]
+        odd_tiles = [jnp.where(low, swapped[i], swapped[i + 1]) for i in range(count + 1)]
         is_odd = jnp.full((8, 128), odd, jnp.int32) == 1
-        lead = [jnp.where(is_odd, odd_tiles[i], even_tiles[i]) for i in range(9)]
-        for i in range(8):
+        lead = [jnp.where(is_odd, odd_tiles[i], even_tiles[i]) for i in range(count + 1)]
+        for i in range(count):
             rows[i, 0:8] = lead[i]
             rows[i, 8:16] = jnp.where(is_odd, even_tiles[i + 1], odd_tiles[i])
             rows[i, 16:24] = lead[i + 1]
         sums = []
-        for i in range(8):
+        for i in range(count):
             summed = weights[0] * rows[i, pl.ds(inner, 8)]
             for tap in range(1, 4):
                 summed = summed + weights[tap] * rows[i, pl.ds(inner + tap, 8)]
@@ -244,7 +249,19 @@
                 remote(swept.at[other], back.at[level, side], channel, in_plane(other, outward), channel + 2).start()
 
     def back_wait(channel):
-        drain(window_0.at[pl.ds(0, 11)], got, channel)
+        drain(window_2.at[pl.ds(0, 11)], got, channel)
+
+    blank = jnp.zeros((8, 128), jnp.float32)
+    for i in (0, 1, 10, 11):
+        ready[i] = blank
+    for i in range(76):
+        strewn[i] = blank
+
+    @pl.when(jnp.logical_and(member > 0, member < 7))
+    def _():
+        for lev in range(2):
+            for part in range(6):
+                back_f[lev, part, 5] = blank
 
     def place_f(lev, part, tile):
         packed_f[lev, part + 1] = tile
@@ -295,27 +312,71 @@
     sweep_y_ahead(plane, range(8), window_1, 27)
     transpose_wait(window_2, 1)
     planes_start(window_2, 4)
+    own_block = 2 * gy + quarter // 2
     drain(window_1.at[pl.ds(0, 40)], got, 2)
 
     for i, tile in enumerate(sweep_x_both()):
-        window_0[OWN + i] = tile
-    planes_start(window_0, 5)
-
-    own_block = 2 * gy + quarter // 2
+        ready[2 + i] = tile
+    start = upstream_x[0, own_block] - 1 + 16 * OWN
+    parts = slide([ready[i] for i in range(12)], start, cubic_weights(fractions[0, 0]))
+    for i, tile in enumerate(parts):
+        strewn[32 + i] = tile
+    for i in range(WINDOW):
+        swept_0[i] = strewn[start // 16 + i]
+
+    def scatter_start(step, others, slot):
+        def start_at(gy_step, side, leave, skip):
+            for other in others:
+                target_plane = lax.rem(plane - step + PLANES, PLANES)
+                copy = remote(
+                    swept_0.at[OWN - 8 * step + other],
+                    back_f.at[level, side, slot],
+                    7,
+                    (target_plane * GROUP + other, lax.rem(gy + gy_step + RING, RING)),
+                    leave,
+                )
+                if skip:
+                    pl.when(other != member)(copy.start)
+                else:
+                    copy.start()
+
+        @pl.when(edge)
+        def _():
+            start_at(outward, jnp.where(quarter == 0, 5, 0), 9, False)
+
+        start_at(0, quarter + 1, 7, step == 0)
+
+    scatter_start(3, (7,), 5)
+    scatter_start(-3, (0,), 5)
+    for step in (2, -2, 1, -1, 0):
+        scatter_start(step, range(GROUP), step + 2)
+    back_f[level, quarter + 1, 2] = swept_0[OWN + member]
+
     planes_wait(window_2, 4)
     for i, tile in enumerate(sweep_x(lambda i: window_2[i], 2, own_block)):
         swept_2[i] = tile
     back_start(swept_2, back_c, 6)
 
-    planes_wait(window_0, 5)
-    for i, tile in enumerate(sweep_x(lambda i: window_0[i], 0, own_block)):
-        swept_0[i] = tile
-    back_start(swept_0, back_f, 7)
-
     back_wait(6)
     coarse = sweep_y(2, lambda i, side: back_c[i // 4, lax.rem(i, 4) + side], 8)
-    back_wait(7)
-    fine = sweep_y(0, lambda i, side: back_f[i // 4, lax.rem(i, 4) + side], 8)
+
+    outer = jnp.logical_or(member == 0, member == 7)
+
+    @pl.when(outer)
+    def _():
+        drain(strewn.at[pl.ds(0, 71)], got, 7)
+
+    @pl.when(jnp.logical_not(outer))
+    def _():
+        drain(strewn.at[pl.ds(0, 59)], got, 7)
+
+    for lev in range(2):
+        for part in range(6):
+            total = back_f[lev, part, 0]
+            for slot in range(1, 6):
+                total = total + back_f[lev, part, slot]
+            ready[lev * 6 + part] = total
+    fine = sweep_y(0, lambda i, side: ready[6 * (i // 4) + lax.rem(i, 4) + side], 8)
     tiles = [a - b for a, b in zip(fine, coarse)]
     for lev in range(2):
         for block in range(2):
@@ -325,17 +386,17 @@
             out_ref[lev, 8:16, columns] = jnp.where(low, swap(even), odd)
 
     drain(cells.at[pl.ds(0, 7)], sent, 0)
-    drain(window_0.at[pl.ds(0, 7)], sent, 1)
-    drain(window_0.at[pl.ds(0, 4)], sent, 3)
+    drain(window_2.at[pl.ds(0, 7)], sent, 1)
+    drain(window_2.at[pl.ds(0, 4)], sent, 3)
     drain(window_1.at[pl.ds(0, 40)], sent, 2)
-    for channel in (4, 5):
-        drain(window_0.at[pl.ds(0, 34)], sent, channel)
-    for channel in (6, 7):
-        drain(window_0.at[pl.ds(0, 7)], sent, channel)
-
-        @pl.when(edge)
-        def _():
-            drain(window_0.at[pl.ds(0, 8)], sent, channel + 2)
+    drain(window_2.at[pl.ds(0, 34)], sent, 4)
+    drain(window_2.at[pl.ds(0, 7)], sent, 6)
+    drain(window_2.at[pl.ds(0, 41)], sent, 7)
+
+    @pl.when(edge)
+    def _():
+        drain(window_2.at[pl.ds(0, 8)], sent, 8)
+        drain(window_2.at[pl.ds(0, 42)], sent, 9)
 
 
 def local(fine_cotangent, coarse_cotangent, upstream_x, upstream_y, fractions):
@@ -363,12 +424,13 @@
             tiles(36),
             tiles(4),
             tiles(63),
+            tiles(12),
+            tiles(76),
             tiles(WINDOW),
             tiles(WINDOW),
-            pltpu.VMEM((8, 24, 128), jnp.float32),
+            pltpu.VMEM((10, 24, 128), jnp.float32),
             tiles(8),
-            tiles(8),
-            tiles(2, 6),
+            tiles(2, 6, 6),
             tiles(2, 6),
             pltpu.SemaphoreType.DMA((10,)),
             pltpu.SemaphoreType.DMA((8,)),

time: 34.9 us -> 33.5 us (0.960)
  Pallas kernels: 34.1 us -> 32.7 us
    pallas_call x1, Pallas kernels: 34.1 us -> 32.7 us  [local(): pl.pallas_call(kernel, out_shape=pltpu.VMEM(fine_cotangent.shape, jnp.flo...]
where the time goes in v3:
time: 33.5 us; the launch traced here: 33.4 us
  Pallas kernels  32.7 us (98%)
  local copies, waits for them, and re-layouts  0.62 us (2%)
    pallas_call x1, Pallas kernels, local(): pl.pallas_call(kernel, out_shape=pltpu.VMEM(fine_cotangent.shape, jnp.flo...  32.7 us

profile of v3, /device:TPU:1, one launch (start us, length us, event | category | flops | bytes accessed | tf_op | source)
XLA Modules:
  0.0 33.4 jit_solution(14321592174089824128)
XLA Ops:
  0.0 32.7 %shard_map.55 = f32[2,16,256]{2,1,0:T(8,128)S(1)} custom-call(f32[2,16,256]{2,1,0:T(8,128)} %fine_hbm.1, f32[2,16,256]{2,1,0:T(8,128)} %coarse_hbm.1, s32[3,8]{1,0:T(4,128)} %upstream_x_hbm.1, s32[3,16]{1,0:T(4,128)} %upstream_y_hbm.1, f32[2,3]{1,0:T(2,128)} %bitcast.1), custom_call_target="tpu_custom_call" | custom-call | tf_op jit(solution)/shard_map/pallas_call | solution.py:409
  32.7 0.6 %copy.7 = f32[2,16,256]{2,1,0:T(8,128)} copy(f32[2,16,256]{2,1,0:T(8,128)S(1)} %shard_map.55) | data formatting | bytes 65536

commit v4 on v3

--- a/solution.py
+++ b/solution.py
@@ -38,7 +38,9 @@
     upstream_y,
     fractions,
     packed_f,
-    packed_c,
+    slabs_c,
+    chosen_c,
+    pencil_c,
     cells,
     edges,
     ahead,
@@ -47,7 +49,6 @@
     ready,
     strewn,
     swept_0,
-    window_2,
     rows,
     swept_2,
     back_f,
@@ -72,7 +73,13 @@
         arrival.start()
     gx, gy = lax.axis_index("gx"), lax.axis_index("gy")
     plane, member = gx // GROUP, lax.rem(gx, GROUP)
-    quarter, level = lax.rem(member, 4), member // 4
+    parity = lax.rem(gy, 2)
+
+    def quarter_of(other, odd):
+        along = lax.rem(other, 4)
+        return along + odd * (1 - 2 * lax.rem(along, 2))
+
+    quarter, level = quarter_of(member, parity), member // 4
     lane = lax.broadcasted_iota(jnp.int32, (8, 128), 1)
     low = lane < HALF
     within = lax.rem(lane, HALF)
@@ -104,6 +111,7 @@
         pl.semaphore_signal(barrier, inc=1, device_id=device, device_id_type=MESH)
 
     edge = jnp.logical_or(quarter == 0, quarter == 3)
+    outer = jnp.logical_or(member == 0, member == GROUP - 1)
     outward = jnp.where(quarter == 0, -1, 1)
     for step in (3, -3, 2, -2, 1, -1):
         greet(up_planes(step))
@@ -125,31 +133,56 @@
                 place(lev, 2 * block, jnp.where(low, upper, swap(lower)))
                 place(lev, 2 * block + 1, jnp.where(low, swap(upper), lower))
 
-    def transpose_start(packed, window, channel):
+    def planes_start(slabs, channel):
+        own = slabs.at[3]
+
+        @pl.when(member == GROUP - 1)
+        def _():
+            remote(own, slabs.at[0], channel, up_planes(3), channel + 4).start()
+
+        @pl.when(member == 0)
+        def _():
+            remote(own, slabs.at[6], channel, up_planes(-3), channel + 4).start()
+
+        for step in (2, -2, 1, -1):
+            remote(own, slabs.at[3 - step], channel, up_planes(step)).start()
+
+    def planes_wait(slabs, channel):
+        @pl.when(outer)
+        def _():
+            drain(slabs.at[pl.ds(0, 5)], got, channel)
+
+        @pl.when(jnp.logical_not(outer))
+        def _():
+            drain(slabs.at[pl.ds(0, 4)], got, channel)
+
+    def choose(slabs, chosen, pass_row):
+        for block in range(2):
+            first = (upstream_x[pass_row, 2 * gy + block] - 1 + 16 * OWN) // 16
+            slab = (first + lax.rem(member + 1 - first + 48, GROUP) + 7) // 8
+            later = jnp.minimum(slab + 1, 6)
+            for lev in range(2):
+                for half in range(2):
+                    tile = 4 * lev + 2 * block + half
+                    chosen[tile, 0] = slabs[slab, tile]
+                    chosen[tile, 1] = slabs[later, tile]
+
+    def transpose_start(chosen, pencil, channel):
         for step in range(1, GROUP):
             other = mate(step)
-            remote(packed.at[other], window.at[OWN + member], channel, in_plane(other)).start()
-        window[OWN + member] = packed[member]
-
-    def transpose_wait(window, channel):
-        drain(window.at[pl.ds(0, 7)], got, channel)
-
-    def planes_start(window, channel):
-        own = window.at[pl.ds(OWN, 8)]
-        remote(window.at[OWN + 7], window.at[0], channel, up_planes(3)).start()
-        remote(window.at[OWN], window.at[WINDOW - 1], channel, up_planes(-3)).start()
-        for step in (2, -2, 1, -1):
-            remote(own, window.at[pl.ds(OWN - 8 * step, 8)], channel, up_planes(step)).start()
-
-    def planes_wait(window, channel):
-        drain(window.at[pl.ds(0, 34)], got, channel)
+            tile = 4 * (other // 4) + quarter_of(other, parity)
+            remote(chosen.at[tile], pencil.at[member], channel, in_plane(other)).start()
+        pencil[member] = chosen[4 * level + quarter]
+
+    def transpose_wait(pencil, channel):
+        drain(pencil.at[pl.ds(0, 7)], got, channel)
 
     def sweep_x(load, pass_row, block):
         shift = upstream_x[pass_row, block]
         weights = cubic_weights(fractions[0, pass_row])
         start = shift - 1 + 16 * OWN
         first = start // 16
-        return slide([load(first + i) for i in range(10)], start, weights)
+        return slide([load(first, i) for i in range(10)], start, weights)
 
     def slide(even_tiles, start, weights):
         count = len(even_tiles) - 2
@@ -212,11 +245,13 @@
         upper_columns = within > crossing + 2
         both = jnp.logical_and(within >= crossing, within <= crossing + 2)
 
-        def load_low(i):
+        def load_low(first, i):
+            i = first + i
             place = 9 * ((i + 7) // 8) + lax.rem(i + 7, 8)
             return jnp.where(upper_columns, 0.0, window_1[place])
 
-        def load_high(i):
+        def load_high(first, i):
+            i = first + i
             level_plane, inside = (i + 7) // 8, lax.rem(i + 7, 8)
             spare = window_1[jnp.where(level_plane == 6, 55, 9 * level_plane + 8)]
             spare = pltpu.roll(spare, lax.rem(crossing - 8 * inside + 256, 128), 1)
@@ -249,7 +284,7 @@
                 remote(swept.at[other], back.at[level, side], channel, in_plane(other, outward), channel + 2).start()
 
     def back_wait(channel):
-        drain(window_2.at[pl.ds(0, 11)], got, channel)
+        drain(strewn.at[pl.ds(0, 11)], got, channel)
 
     blank = jnp.zeros((8, 128), jnp.float32)
     for i in (0, 1, 10, 11):
@@ -267,7 +302,7 @@
         packed_f[lev, part + 1] = tile
 
     def place_c(lev, part, tile):
-        packed_c[4 * lev + part] = tile
+        slabs_c[3, 4 * lev + part] = tile
 
     for lev in range(2):
         packed_f[lev, 0] = jnp.zeros((8, 128), jnp.float32)
@@ -277,16 +312,16 @@
     pl.semaphore_wait(barrier, 17)
 
     for lev in range(2):
-        remote(packed_f.at[lev, 4], edges.at[member], 3, in_plane(4 * lev, 1)).start()
-        remote(packed_f.at[lev, 1], edges.at[member], 3, in_plane(4 * lev + 3, -1)).start()
+        remote(packed_f.at[lev, 4], edges.at[member], 3, in_plane(4 * lev + 1 - parity, 1)).start()
+        remote(packed_f.at[lev, 1], edges.at[member], 3, in_plane(4 * lev + 2 + parity, -1)).start()
     for step in range(1, GROUP):
         other = mate(step)
-        source = packed_f.at[other // 4, pl.ds(lax.rem(other, 4), 3)]
+        source = packed_f.at[other // 4, pl.ds(quarter_of(other, parity), 3)]
         remote(source, cells.at[member], 0, in_plane(other)).start()
     cells[member] = packed_f[level, pl.ds(quarter, 3)]
     arrivals[4].wait()
     pack(coarse_ref, place_c)
-    transpose_start(packed_c, window_2, 1)
+    planes_start(slabs_c, 1)
     for arrival in arrivals[1:4]:
         arrival.wait()
     drain(cells.at[pl.ds(0, 7)], got, 0)
@@ -310,9 +345,16 @@
         target = window_1.at[pl.ds(9 * (3 - step), 9)]
         remote(ahead.at[pl.ds(9 * n, 9)], target, 2, up_planes(step)).start()
     sweep_y_ahead(plane, range(8), window_1, 27)
-    transpose_wait(window_2, 1)
-    planes_start(window_2, 4)
+    planes_wait(slabs_c, 1)
+    choose(slabs_c, chosen_c, 2)
+    transpose_start(chosen_c, pencil_c, 4)
     own_block = 2 * gy + quarter // 2
+    transpose_wait(pencil_c, 4)
+    coarse_rows = sweep_x(lambda first, i: pencil_c[lax.rem(first + i + 7, 8), i // 8], 2, own_block)
+    for i, tile in enumerate(coarse_rows):
+        swept_2[i] = tile
+    back_start(swept_2, back_c, 6)
+
     drain(window_1.at[pl.ds(0, 40)], got, 2)
 
     for i, tile in enumerate(sweep_x_both()):
@@ -324,7 +366,7 @@
     for i in range(WINDOW):
         swept_0[i] = strewn[start // 16 + i]
 
-    def scatter_start(step, others, slot):
+    def scatter_start(step, others, slot, outer_gy):
         def start_at(gy_step, side, leave, skip):
             for other in others:
                 target_plane = lax.rem(plane - step + PLANES, PLANES)
@@ -340,27 +382,22 @@
                 else:
                     copy.start()
 
-        @pl.when(edge)
-        def _():
-            start_at(outward, jnp.where(quarter == 0, 5, 0), 9, False)
-
-        start_at(0, quarter + 1, 7, step == 0)
-
-    scatter_start(3, (7,), 5)
-    scatter_start(-3, (0,), 5)
-    for step in (2, -2, 1, -1, 0):
-        scatter_start(step, range(GROUP), step + 2)
+        if outer_gy:
+            @pl.when(edge)
+            def _():
+                start_at(outward, jnp.where(quarter == 0, 5, 0), 9, False)
+        else:
+            start_at(0, quarter + 1, 7, step == 0)
+
+    for outer_gy in (True, False):
+        scatter_start(3, (7,), 5, outer_gy)
+        scatter_start(-3, (0,), 5, outer_gy)
+        for step in (2, -2, 1, -1, 0):
+            scatter_start(step, range(GROUP), step + 2, outer_gy)
     back_f[level, quarter + 1, 2] = swept_0[OWN + member]
-
-    planes_wait(window_2, 4)
-    for i, tile in enumerate(sweep_x(lambda i: window_2[i], 2, own_block)):
-        swept_2[i] = tile
-    back_start(swept_2, back_c, 6)
 
     back_wait(6)
     coarse = sweep_y(2, lambda i, side: back_c[i // 4, lax.rem(i, 4) + side], 8)
-
-    outer = jnp.logical_or(member == 0, member == 7)
 
     @pl.when(outer)
     def _():
@@ -386,17 +423,22 @@
             out_ref[lev, 8:16, columns] = jnp.where(low, swap(even), odd)
 
     drain(cells.at[pl.ds(0, 7)], sent, 0)
-    drain(window_2.at[pl.ds(0, 7)], sent, 1)
-    drain(window_2.at[pl.ds(0, 4)], sent, 3)
+    drain(slabs_c.at[pl.ds(0, 4)], sent, 1)
+
+    @pl.when(outer)
+    def _():
+        drain(slabs_c.at[0], sent, 5)
+
+    drain(strewn.at[pl.ds(0, 4)], sent, 3)
     drain(window_1.at[pl.ds(0, 40)], sent, 2)
-    drain(window_2.at[pl.ds(0, 34)], sent, 4)
-    drain(window_2.at[pl.ds(0, 7)], sent, 6)
-    drain(window_2.at[pl.ds(0, 41)], sent, 7)
+    drain(pencil_c.at[pl.ds(0, 7)], sent, 4)
+    drain(strewn.at[pl.ds(0, 7)], sent, 6)
+    drain(strewn.at[pl.ds(0, 41)], sent, 7)
 
     @pl.when(edge)
     def _():
-        drain(window_2.at[pl.ds(0, 8)], sent, 8)
-        drain(window_2.at[pl.ds(0, 42)], sent, 9)
+        drain(strewn.at[pl.ds(0, 8)], sent, 8)
+        drain(strewn.at[pl.ds(0, 42)], sent, 9)
 
 
 def local(fine_cotangent, coarse_cotangent, upstream_x, upstream_y, fractions):
@@ -418,7 +460,9 @@
             pltpu.SMEM(upstream_y.shape, jnp.int32),
             pltpu.SMEM((2, 3), jnp.float32),
             tiles(2, 6),
-            tiles(GROUP),
+            tiles(7, 8),
+            tiles(8, 2),
+            tiles(8, 2),
             tiles(8, 3),
             tiles(8),
             tiles(36),
@@ -426,7 +470,6 @@
             tiles(63),
             tiles(12),
             tiles(76),
-            tiles(WINDOW),
             tiles(WINDOW),
             pltpu.VMEM((10, 24, 128), jnp.float32),
             tiles(8),

time: 33.5 us -> 32.9 us (0.982)
  Pallas kernels: 32.7 us -> 32.1 us
    pallas_call x1, Pallas kernels: 32.7 us -> 32.1 us  [local(): pl.pallas_call(kernel, out_shape=pltpu.VMEM(fine_cotangent.shape, jnp.flo...]
where the time goes in v4:
time: 32.9 us; the launch traced here: 32.8 us
  Pallas kernels  32.1 us (98%)
  local copies, waits for them, and re-layouts  0.62 us (2%)
    pallas_call x1, Pallas kernels, local(): pl.pallas_call(kernel, out_shape=pltpu.VMEM(fine_cotangent.shape, jnp.flo...  32.1 us

profile of v4, /device:TPU:1, one launch (start us, length us, event | category | flops | bytes accessed | tf_op | source)
XLA Modules:
  0.0 32.8 jit_solution(13885222969433170005)
XLA Ops:
  0.0 32.1 %shard_map.55 = f32[2,16,256]{2,1,0:T(8,128)S(1)} custom-call(f32[2,16,256]{2,1,0:T(8,128)} %fine_hbm.1, f32[2,16,256]{2,1,0:T(8,128)} %coarse_hbm.1, s32[3,8]{1,0:T(4,128)} %upstream_x_hbm.1, s32[3,16]{1,0:T(4,128)} %upstream_y_hbm.1, f32[2,3]{1,0:T(2,128)} %bitcast.1), custom_call_target="tpu_custom_call" | custom-call | tf_op jit(solution)/shard_map/pallas_call | solution.py:451
  32.1 0.6 %copy.7 = f32[2,16,256]{2,1,0:T(8,128)} copy(f32[2,16,256]{2,1,0:T(8,128)S(1)} %shard_map.55) | data formatting | bytes 65536

commit v5 on v4

--- a/solution.py
+++ b/solution.py
@@ -42,14 +42,17 @@
     chosen_c,
     pencil_c,
     cells,
+    mixed,
     edges,
     ahead,
     fringe,
     window_1,
+    taps,
     ready,
     strewn,
     swept_0,
     rows,
+    rows_high,
     swept_2,
     back_f,
     back_c,
@@ -69,8 +72,7 @@
             )
         )
     ]
-    for arrival in arrivals:
-        arrival.start()
+    arrivals[0].start()
     gx, gy = lax.axis_index("gx"), lax.axis_index("gy")
     plane, member = gx // GROUP, lax.rem(gx, GROUP)
     parity = lax.rem(gy, 2)
@@ -123,6 +125,8 @@
 
     for step in range(1, GROUP):
         greet(in_plane(mate(step)))
+    for arrival in arrivals[1:]:
+        arrival.start()
 
     def pack(field, place):
         for lev in range(2):
@@ -132,6 +136,9 @@
                 lower = field[lev, 8:16, columns]
                 place(lev, 2 * block, jnp.where(low, upper, swap(lower)))
                 place(lev, 2 * block + 1, jnp.where(low, swap(upper), lower))
+
+    def weights_of(pass_row, direction):
+        return [taps[2 * pass_row + direction, tap] for tap in range(4)]
 
     def planes_start(slabs, channel):
         own = slabs.at[3]
@@ -177,14 +184,14 @@
     def transpose_wait(pencil, channel):
         drain(pencil.at[pl.ds(0, 7)], got, channel)
 
-    def sweep_x(load, pass_row, block):
+    def sweep_x(load, pass_row, block, rows=rows):
         shift = upstream_x[pass_row, block]
-        weights = cubic_weights(fractions[0, pass_row])
+        weights = weights_of(pass_row, 0)
         start = shift - 1 + 16 * OWN
         first = start // 16
-        return slide([load(first, i) for i in range(10)], start, weights)
-
-    def slide(even_tiles, start, weights):
+        return slide([load(first, i) for i in range(10)], start, weights, rows)
+
+    def slide(even_tiles, start, weights, rows=rows):
         count = len(even_tiles) - 2
         odd, inner = lax.rem(start // 8, 2), lax.rem(start, 8)
         swapped = [swap(tile) for tile in even_tiles]
@@ -219,25 +226,36 @@
     def crossing_of(to_plane):
         return border - upstream_y[1, to_plane] - 2
 
+    def mix_ahead():
+        weights = weights_of(1, 1)
+        blank_tile = jnp.zeros((8, 128), jnp.float32)
+        kept, split_off = {}, {}
+        for side in range(2):
+            for tap in range(1, 4):
+                split = jnp.logical_and(within + tap >= HALF, lax.rem(quarter, 2) == side)
+                kept[side, tap] = jnp.where(split, 0.0, weights[tap])
+                split_off[side, tap] = jnp.where(split, weights[tap], 0.0)
+        spare = blank_tile
+        for i in range(8):
+            second = blank_tile
+            for side in range(3):
+                main = weights[0] * cells[i, side]
+                for tap in range(1, 4):
+                    moved = pltpu.roll(cells[i, side], 128 - tap, 1)
+                    if side == 2:
+                        main = main + weights[tap] * moved
+                        continue
+                    moved = jnp.where(within + tap < HALF, moved, pltpu.roll(cells[i, side + 1], HALF - tap, 1))
+                    main = main + kept[side, tap] * moved
+                    second = second + split_off[side, tap] * moved
+                mixed[i, side] = main
+            spare = spare + pltpu.roll(second, (8 * i - 61) % 128, 1)
+        return spare
+
     def sweep_y_ahead(to_plane, tiles, target, at):
-        shift = upstream_y[1, to_plane]
-        crossing = crossing_of(to_plane)
-        upper_columns = within > crossing + 2
-        spare = jnp.zeros((8, 128), jnp.float32)
-        parts = []
-        for tap, weight in enumerate(cubic_weights(fractions[1, 1])):
-            offset = shift - 1 + tap
-            split = jnp.logical_and(within + offset >= border, jnp.logical_not(upper_columns))
-            parts.append((offset, jnp.where(split, 0.0, weight), jnp.where(split, weight, 0.0)))
+        offset = upstream_y[1, to_plane] - 1
         for n, i in enumerate(tiles):
-            main = jnp.zeros((8, 128), jnp.float32)
-            second = jnp.zeros((8, 128), jnp.float32)
-            for offset, first_weight, second_weight in parts:
-                moved = shifted_cells(lambda i, side: cells[i, side], i, offset)
-                main = main + first_weight * moved
-                second = second + second_weight * moved
-            target[at + n] = main
-            spare = spare + pltpu.roll(second, lax.rem(8 * i - crossing + 256, 128), 1)
+            target[at + n] = shifted_cells(lambda i, side: mixed[i, side], i, offset)
         target[at + len(tiles)] = spare
 
     def sweep_x_both():
@@ -258,12 +276,12 @@
             return jnp.where(upper_columns, window_1[9 * level_plane + inside], jnp.where(both, spare, 0.0))
 
         low_part = sweep_x(load_low, 1, low_block)
-        high_part = sweep_x(load_high, 1, high_block)
+        high_part = sweep_x(load_high, 1, high_block, rows_high)
         return [a + b for a, b in zip(low_part, high_part)]
 
     def sweep_y(pass_row, load, count):
         shift = upstream_y[pass_row, plane]
-        weights = cubic_weights(fractions[1, pass_row])
+        weights = weights_of(pass_row, 1)
         sums = [None] * count
         for tap in range(4):
             for i in range(count):
@@ -324,6 +342,10 @@
     planes_start(slabs_c, 1)
     for arrival in arrivals[1:4]:
         arrival.wait()
+    for pass_row in range(3):
+        for direction in range(2):
+            for tap, weight in enumerate(cubic_weights(fractions[direction, pass_row])):
+                taps[2 * pass_row + direction, tap] = weight
     drain(cells.at[pl.ds(0, 7)], got, 0)
 
     @pl.when(edge)
@@ -336,6 +358,7 @@
     def to(step):
         return lax.rem(plane + step + PLANES, PLANES)
 
+    spare = mix_ahead()
     sweep_y_ahead(to(3), (7,), fringe, 0)
     remote(fringe.at[pl.ds(0, 2)], window_1.at[pl.ds(7, 2)], 2, up_planes(3)).start()
     sweep_y_ahead(to(-3), (0,), fringe, 2)
@@ -360,7 +383,7 @@
     for i, tile in enumerate(sweep_x_both()):
         ready[2 + i] = tile
     start = upstream_x[0, own_block] - 1 + 16 * OWN
-    parts = slide([ready[i] for i in range(12)], start, cubic_weights(fractions[0, 0]))
+    parts = slide([ready[i] for i in range(12)], start, weights_of(0, 0))
     for i, tile in enumerate(parts):
         strewn[32 + i] = tile
     for i in range(WINDOW):
@@ -392,12 +415,31 @@
     for outer_gy in (True, False):
         scatter_start(3, (7,), 5, outer_gy)
         scatter_start(-3, (0,), 5, outer_gy)
+    for outer_gy in (True, False):
         for step in (2, -2, 1, -1, 0):
             scatter_start(step, range(GROUP), step + 2, outer_gy)
     back_f[level, quarter + 1, 2] = swept_0[OWN + member]
 
     back_wait(6)
     coarse = sweep_y(2, lambda i, side: back_c[i // 4, lax.rem(i, 4) + side], 8)
+
+    drain(cells.at[pl.ds(0, 7)], sent, 0)
+    drain(slabs_c.at[pl.ds(0, 4)], sent, 1)
+
+    @pl.when(outer)
+    def _():
+        drain(slabs_c.at[0], sent, 5)
+
+    drain(strewn.at[pl.ds(0, 4)], sent, 3)
+    drain(window_1.at[pl.ds(0, 40)], sent, 2)
+    drain(pencil_c.at[pl.ds(0, 7)], sent, 4)
+    drain(strewn.at[pl.ds(0, 7)], sent, 6)
+    drain(strewn.at[pl.ds(0, 41)], sent, 7)
+
+    @pl.when(edge)
+    def _():
+        drain(strewn.at[pl.ds(0, 8)], sent, 8)
+        drain(strewn.at[pl.ds(0, 42)], sent, 9)
 
     @pl.when(outer)
     def _():
@@ -421,24 +463,6 @@
             even, odd = tiles[lev * 4 + 2 * block], tiles[lev * 4 + 2 * block + 1]
             out_ref[lev, 0:8, columns] = jnp.where(low, even, swap(odd))
             out_ref[lev, 8:16, columns] = jnp.where(low, swap(even), odd)
-
-    drain(cells.at[pl.ds(0, 7)], sent, 0)
-    drain(slabs_c.at[pl.ds(0, 4)], sent, 1)
-
-    @pl.when(outer)
-    def _():
-        drain(slabs_c.at[0], sent, 5)
-
-    drain(strewn.at[pl.ds(0, 4)], sent, 3)
-    drain(window_1.at[pl.ds(0, 40)], sent, 2)
-    drain(pencil_c.at[pl.ds(0, 7)], sent, 4)
-    drain(strewn.at[pl.ds(0, 7)], sent, 6)
-    drain(strewn.at[pl.ds(0, 41)], sent, 7)
-
-    @pl.when(edge)
-    def _():
-        drain(strewn.at[pl.ds(0, 8)], sent, 8)
-        drain(strewn.at[pl.ds(0, 42)], sent, 9)
 
 
 def local(fine_cotangent, coarse_cotangent, upstream_x, upstream_y, fractions):
@@ -464,13 +488,16 @@
             tiles(8, 2),
             tiles(8, 2),
             tiles(8, 3),
+            tiles(8, 3),
             tiles(8),
             tiles(36),
             tiles(4),
             tiles(63),
+            tiles(6, 4),
             tiles(12),
             tiles(76),
             tiles(WINDOW),
+            pltpu.VMEM((10, 24, 128), jnp.float32),
             pltpu.VMEM((10, 24, 128), jnp.float32),
             tiles(8),
             tiles(2, 6, 6),

time: 32.9 us -> 32.7 us (level)
  no operation moved by 1% of the time
where the time goes in v5:
time: 32.7 us; the launch traced here: 32.6 us
  Pallas kernels  31.9 us (98%)
  local copies, waits for them, and re-layouts  0.62 us (2%)
    pallas_call x1, Pallas kernels, local(): pl.pallas_call(kernel, out_shape=pltpu.VMEM(fine_cotangent.shape, jnp.flo...  31.9 us

profile of v5, /device:TPU:1, one launch (start us, length us, event | category | flops | bytes accessed | tf_op | source)
XLA Modules:
  0.0 32.6 jit_solution(14950663206831988279)
XLA Ops:
  0.0 31.9 %shard_map.55 = f32[2,16,256]{2,1,0:T(8,128)S(1)} custom-call(f32[2,16,256]{2,1,0:T(8,128)} %fine_hbm.1, f32[2,16,256]{2,1,0:T(8,128)} %coarse_hbm.1, s32[3,8]{1,0:T(4,128)} %upstream_x_hbm.1, s32[3,16]{1,0:T(4,128)} %upstream_y_hbm.1, f32[2,3]{1,0:T(2,128)} %bitcast.1), custom_call_target="tpu_custom_call" | custom-call | tf_op jit(solution)/shard_map/pallas_call | solution.py:475
  32.0 0.6 %copy.7 = f32[2,16,256]{2,1,0:T(8,128)} copy(f32[2,16,256]{2,1,0:T(8,128)S(1)} %shard_map.55) | data formatting | bytes 65536

commit v6 on v5

--- a/solution.py
+++ b/solution.py
@@ -359,14 +359,19 @@
         return lax.rem(plane + step + PLANES, PLANES)
 
     spare = mix_ahead()
+    def send_ahead(n, step):
+        sweep_y_ahead(to(step), range(8), ahead, 9 * n)
+        target = window_1.at[pl.ds(9 * (3 - step), 9)]
+        remote(ahead.at[pl.ds(9 * n, 9)], target, 2, up_planes(step)).start()
+
+    send_ahead(0, 2)
+    send_ahead(1, -2)
     sweep_y_ahead(to(3), (7,), fringe, 0)
     remote(fringe.at[pl.ds(0, 2)], window_1.at[pl.ds(7, 2)], 2, up_planes(3)).start()
     sweep_y_ahead(to(-3), (0,), fringe, 2)
     remote(fringe.at[pl.ds(2, 2)], window_1.at[pl.ds(54, 2)], 2, up_planes(-3)).start()
-    for n, step in enumerate((2, -2, 1, -1)):
-        sweep_y_ahead(to(step), range(8), ahead, 9 * n)
-        target = window_1.at[pl.ds(9 * (3 - step), 9)]
-        remote(ahead.at[pl.ds(9 * n, 9)], target, 2, up_planes(step)).start()
+    send_ahead(2, 1)
+    send_ahead(3, -1)
     sweep_y_ahead(plane, range(8), window_1, 27)
     planes_wait(slabs_c, 1)
     choose(slabs_c, chosen_c, 2)

time: 32.7 us -> 32.5 us (level)
  no operation moved by 1% of the time
where the time goes in v6:
time: 32.5 us; the launch traced here: 32.4 us
  Pallas kernels  31.7 us (98%)
  local copies, waits for them, and re-layouts  0.62 us (2%)
    pallas_call x1, Pallas kernels, local(): pl.pallas_call(kernel, out_shape=pltpu.VMEM(fine_cotangent.shape, jnp.flo...  31.7 us

profile of v6, /device:TPU:1, one launch (start us, length us, event | category | flops | bytes accessed | tf_op | source)
XLA Modules:
  0.0 32.4 jit_solution(8169200695808334001)
XLA Ops:
  0.0 31.7 %shard_map.55 = f32[2,16,256]{2,1,0:T(8,128)S(1)} custom-call(f32[2,16,256]{2,1,0:T(8,128)} %fine_hbm.1, f32[2,16,256]{2,1,0:T(8,128)} %coarse_hbm.1, s32[3,8]{1,0:T(4,128)} %upstream_x_hbm.1, s32[3,16]{1,0:T(4,128)} %upstream_y_hbm.1, f32[2,3]{1,0:T(2,128)} %bitcast.1), custom_call_target="tpu_custom_call" | custom-call | tf_op jit(solution)/shard_map/pallas_call | solution.py:480
  31.7 0.6 %copy.7 = f32[2,16,256]{2,1,0:T(8,128)} copy(f32[2,16,256]{2,1,0:T(8,128)S(1)} %shard_map.55) | data formatting | bytes 65536

commit v7 on v6

--- a/solution.py
+++ b/solution.py
@@ -305,16 +305,6 @@
         drain(strewn.at[pl.ds(0, 11)], got, channel)
 
     blank = jnp.zeros((8, 128), jnp.float32)
-    for i in (0, 1, 10, 11):
-        ready[i] = blank
-    for i in range(76):
-        strewn[i] = blank
-
-    @pl.when(jnp.logical_and(member > 0, member < 7))
-    def _():
-        for lev in range(2):
-            for part in range(6):
-                back_f[lev, part, 5] = blank
 
     def place_f(lev, part, tile):
         packed_f[lev, part + 1] = tile
@@ -340,6 +330,17 @@
     arrivals[4].wait()
     pack(coarse_ref, place_c)
     planes_start(slabs_c, 1)
+    for i in (0, 1, 10, 11):
+        ready[i] = blank
+    for i in range(76):
+        strewn[i] = blank
+
+    @pl.when(jnp.logical_and(member > 0, member < 7))
+    def _():
+        for lev in range(2):
+            for part in range(6):
+                back_f[lev, part, 5] = blank
+
     for arrival in arrivals[1:4]:
         arrival.wait()
     for pass_row in range(3):

time: 32.5 us -> 32.5 us (level)
  no operation moved by 1% of the time
where the time goes in v7:
time: 32.5 us; the launch traced here: 32.4 us
  Pallas kernels  31.7 us (98%)
  local copies, waits for them, and re-layouts  0.62 us (2%)
    pallas_call x1, Pallas kernels, local(): pl.pallas_call(kernel, out_shape=pltpu.VMEM(fine_cotangent.shape, jnp.flo...  31.7 us

profile of v7, /device:TPU:1, one launch (start us, length us, event | category | flops | bytes accessed | tf_op | source)
XLA Modules:
  0.0 32.4 jit_solution(9897307708308484469)
XLA Ops:
  0.0 31.7 %shard_map.55 = f32[2,16,256]{2,1,0:T(8,128)S(1)} custom-call(f32[2,16,256]{2,1,0:T(8,128)} %fine_hbm.1, f32[2,16,256]{2,1,0:T(8,128)} %coarse_hbm.1, s32[3,8]{1,0:T(4,128)} %upstream_x_hbm.1, s32[3,16]{1,0:T(4,128)} %upstream_y_hbm.1, f32[2,3]{1,0:T(2,128)} %bitcast.1), custom_call_target="tpu_custom_call" | custom-call | tf_op jit(solution)/shard_map/pallas_call | solution.py:481
  31.7 0.6 %copy.7 = f32[2,16,256]{2,1,0:T(8,128)} copy(f32[2,16,256]{2,1,0:T(8,128)S(1)} %shard_map.55) | data formatting | bytes 65536
